TPU v7x, 32 devices: a whole 2x2x4 slice. The times are simulated.
32 devices in a mesh: lat: 8 (over z, y), orient: 4 (over x, core).
Axes of the slice: x: 2, y: 2, z: 4, core: 2. Of those that a mesh axis runs over, the one named last changes fastest.
Arguments:
- features: bfloat16 [16, 32, 32, 8192], P('orient', None, 'lat'), may hold values from -6 to 6
- mix_weights: bfloat16 [2, 3, 32, 32], replicated, may hold values from -0.625 to 0.625
- kernels: bfloat16 [2, 9, 32, 32], replicated, may hold values from -0.375 to 0.375
- bias_terms: float32 [2, 32], replicated, may hold values from -3 to 3
Outputs:
- responses: bfloat16 [16, 32, 32, 8192], P('orient', None, 'lat')
All inputs are finite; a program needn't handle non-finite values.
Results may differ from a plain program's by a relative error of at most 0.0061.
Values may be sent and summed in bfloat16 or wider, within the bound.
No kernel may reach another device: no remote copies, remote signals or barrier semaphores. Data moves between devices by JAX's collectives and lax.ppermute only.
A program may use at most 128 MiB of HBM per device.

v0:
```python
import jax
import jax.numpy as jnp
import numpy as np
from jax import lax
from jax.sharding import PartitionSpec as P

LAYERS = 2


CYCLE_PLACE = np.array([0, 1, 2, 7, -1, 3, 6, 5, 4])
CYCLE_PAIRS = np.outer((CYCLE_PLACE >= 0).astype(np.float32), (CYCLE_PLACE >= 0).astype(np.float32))
CENTER_ONE = np.outer((CYCLE_PLACE < 0).astype(np.float32), (CYCLE_PLACE < 0).astype(np.float32))


def extended_2(block, sides, width, periodic):
    for axis, dim in sides:
        count = lax.axis_size(axis)
        forward = [(i, i + 1) for i in range(count - 1)]
        if periodic:
            forward.append((count - 1, 0))
        backward = [(target, source) for source, target in forward]
        low = lax.ppermute(
            lax.slice_in_dim(block, block.shape[dim] - width, None, axis=dim), axis, forward
        )
        high = lax.ppermute(lax.slice_in_dim(block, 0, width, axis=dim), axis, backward)
        block = jnp.concatenate([low, block, high], axis=dim)
    return block


def rotation_table(orient):
    half_turn = orient.astype(jnp.float32) * 0.5
    positions = jnp.asarray(CYCLE_PLACE).astype(jnp.float32)
    distance = jnp.mod(positions[:, None] - positions[None, :] - half_turn + 4.0, 8.0) - 4.0
    weight = jnp.maximum(0.0, 1.0 - jnp.abs(distance))
    return weight * jnp.asarray(CYCLE_PAIRS).astype(jnp.float32) + jnp.asarray(CENTER_ONE).astype(
        jnp.float32
    )


def rotated_kernels(kernel, orient):
    table = rotation_table(orient)
    return jnp.einsum(
        "ab,bij->aij", table, kernel.astype(jnp.float32), precision=lax.Precision.HIGHEST
    ).astype(jnp.bfloat16)


def mix_orients(extended, mixing, count):
    running = None
    for offset in range(3):
        term = jnp.einsum(
            "ij,ojrw->oirw",
            mixing[offset],
            extended[offset : offset + count],
            preferred_element_type=jnp.float32,
        )
        running = term if running is None else running + term
    return running.astype(jnp.bfloat16)


def conv_layer(padded, rotated, bias_row, out_rows):
    row_stack = jnp.stack(
        [padded[:, :, row_start : row_start + out_rows, :] for row_start in range(3)], axis=1
    )
    running = None
    for col_index in range(3):
        col_shift = col_index - 1
        taps = rotated[:, col_index::3]
        term = jnp.einsum("otij,otjrw->oirw", taps, row_stack, preferred_element_type=jnp.float32)
        term = jnp.roll(term, -col_shift, axis=3)
        running = term if running is None else running + term
    return jax.nn.relu(running + bias_row[None, :, None, None]).astype(jnp.bfloat16)


def local(features, mix_weights, kernels, bias_terms):
    count = features.shape[0]
    rows = features.shape[2]
    orients_here = lax.axis_index("orient") * count + jnp.arange(count, dtype=jnp.int32)
    rotations = [
        jax.vmap(lambda orient, kernel=kernels[layer_index]: rotated_kernels(kernel, orient))(
            orients_here
        )
        for layer_index in range(LAYERS)
    ]
    current = features
    for layer_index in range(LAYERS):
        extended = extended_2(current, (("orient", 0),), 1, True)
        mixed_feats = mix_orients(extended, mix_weights[layer_index], count)
        padded = extended_2(mixed_feats, (("lat", 2),), 1, False)
        current = conv_layer(padded, rotations[layer_index], bias_terms[layer_index], rows)
    return current


def solution(mesh):
    in_specs = (P("orient", None, "lat", None), P(), P(), P())
    out_specs = P("orient", None, "lat", None)
    return jax.shard_map(local, mesh=mesh, in_specs=in_specs, out_specs=out_specs, check_vma=False)
```

profile of v0, /device:TPU:19, one launch (start us, length us, event | category | flops | bytes accessed | tf_op | source)
XLA Modules:
  0.0 510.7 jit_solution(17306025618806973547)
XLA Ops:
  0.0 11.4 %copy.10 = bf16[4,32,4,8192]{3,1,2,0:T(8,128)(2,1)} copy(bf16[4,32,4,8192]{3,2,1,0:T(4,128)(2,1)} %param.7) | data formatting | bytes 16777216 | tf_op args[0]
  11.4 4.9 fusion.116
  16.3 0.8 collective-permute-start
  17.2 0.5 collective-permute-start.1
  17.7 0.0 copy-done.5
  17.7 0.0 copy-done.1
  17.7 17.6 %fusion.89 = f32[4,4,8192,32]{2,3,1,0:T(8,128)} fusion(bf16[2,3,32,32]{3,2,1,0:T(8,128)(2,1)S(1)} %copy-done.5, bf16[4,32,4,8192]{3,2,1,0:T(4,128)(2,1)S(1)} %copy-done.1), kind=kOutput, calls=%fused_computation.95 | convolution fusion | flops 268435456 | bytes 25174016 | tf_op jit(solution)/shard_map/ij,ojrw->oirw/dot_general | solution.py:50
  35.3 25.3 %collective-permute-done = bf16[1,32,4,8192]{3,1,2,0:T(8,128)(2,1)} collective-permute-done((bf16[1,32,4,8192]{3,1,2,0:T(8,128)(2,1)}, bf16[1,32,4,8192]{3,1,2,0:T(8,128)(2,1)}, u32[]{:S(2)}, u32[]{:S(2)}) %collective-permute-start) | collective-permute-done | bytes 2097184 | tf_op jit(solution)/shard_map/ppermute | solution.py:22
  60.6 0.0 slice-done
  60.6 9.9 %fusion.46 = f32[4,4,8192,32]{2,3,1,0:T(8,128)} fusion(bf16[4,32,4,8192]{3,1,2,0:T(8,128)(2,1)S(1)} %bitcast.102, bf16[1,32,4,8192]{3,1,2,0:T(8,128)(2,1)} %collective-permute-done, bf16[2,3,32,32]{3,2,1,0:T(8,128)(2,1)S(1)} %copy-done.5), kind=kOutput, calls=%fused_computation.48 | convolution fusion | flops 285212672 | bytes 27271168 | tf_op jit(solution)/shard_map/ij,ojrw->oirw/dot_general | solution.py:50
  70.4 0.0 collective-permute-done.1
  70.4 17.0 %add_convert_fusion.1 = bf16[4,4,8192,32]{2,3,1,0:T(8,128)(2,1)} fusion(f32[4,4,8192,32]{2,3,1,0:T(8,128)} %fusion.46, f32[4,4,8192,32]{2,3,1,0:T(8,128)} %fusion.89, bf16[1,32,4,8192]{3,1,2,0:T(8,128)(2,1)S(1)} %collective-permute-done.1, bf16[4,32,4,8192]{3,1,2,0:T(8,128)(2,1)} %copy.10, bf16[2,3,32,32]{3,2,1,0:T(8,128)(2,1)S(1)} %copy-done.5), kind=kOutput, calls=%fused_computation.25 | convolution fusion | flops 297795584 | bytes 52436992 | tf_op jit(solution)/shard_map/ij,ojrw->oirw/dot_general | solution.py:50
  87.5 0.0 copy-start.6
  87.5 0.0 copy-start.7
  87.5 0.0 copy-start.10
  87.5 4.8 fusion.115
  92.3 3.1 collective-permute-start.2
  95.4 3.0 collective-permute-start.3
  98.5 0.1 broadcast_add_fusion
  98.6 0.6 convolution_convert_fusion
  99.3 0.4 slice.164
  99.7 0.4 slice.149
  100.1 0.4 slice.163
  100.5 0.0 slice-start.2
  100.5 0.5 slice_bitcast_fusion
  101.0 81.3 %collective-permute-done.2 = bf16[4,32,1,8192]{3,1,2,0:T(8,128)(2,1)S(1)} collective-permute-done((bf16[4,32,1,8192]{3,1,2,0:T(8,128)(2,1)}, bf16[4,32,1,8192]{3,1,2,0:T(8,128)(2,1)S(1)}, u32[]{:S(2)}, u32[]{:S(2)}) %collective-permute-start.2) | collective-permute-done | bytes 2097184 | tf_op jit(solution)/shard_map/ppermute | solution.py:22
  182.3 5.6 %collective-permute-done.3 = bf16[4,32,1,8192]{3,1,2,0:T(8,128)(2,1)} collective-permute-done((bf16[4,32,1,8192]{3,1,2,0:T(8,128)(2,1)}, bf16[4,32,1,8192]{3,1,2,0:T(8,128)(2,1)}, u32[]{:S(2)}, u32[]{:S(2)}) %collective-permute-start.3) | collective-permute-done | bytes 2097184 | tf_op jit(solution)/shard_map/ppermute | solution.py:25
  187.9 10.8 %fusion.43 = (bf16[4,1,32,4,8192]{4,2,3,0,1:T(8,128)(2,1)}, bf16[4,1,32,4,8192]{4,2,3,0,1:T(8,128)(2,1)}) fusion(bf16[4,32,4,8192]{3,1,2,0:T(8,128)(2,1)} %bitcast.104, bf16[4,32,1,8192]{3,1,2,0:T(8,128)(2,1)S(1)} %collective-permute-done.2, bf16[4,32,1,8192]{3,1,2,0:T(8,128)(2,1)} %collective-permute-done.3), kind=kLoop, calls=%fused_computation.43 | loop fusion | flops 8388608 | bytes 29360128 | tf_op jit(solution)/shard_map/stack | solution.py:61
  198.7 0.0 slice-done.3
  198.7 9.8 %fusion.25 = f32[4,32,4,8192]{3,1,2,0:T(8,128)S(1)} fusion(bf16[4,3,32,32,1]{3,1,2,0,4:T(4,128)(2,1)S(1)} %bitcast.121, bf16[4,1,32,4,8192]{4,2,3,0,1:T(8,128)(2,1)} %get-tuple-element.12, bf16[4,1,32,4,8192]{4,2,3,0,1:T(8,128)(2,1)S(1)} %bitcast.108, bf16[4,1,32,4,8192]{4,2,3,0,1:T(8,128)(2,1)} %get-tuple-element.11), kind=kOutput, calls=%fused_computation.27 | convolution fusion | flops 830472192 | bytes 41967616 | tf_op jit(solution)/shard_map/otij,otjrw->oirw/dot_general | solution.py:68
  208.5 9.1 %slice.192 = f32[4,32,4,8191]{3,1,2,0:T(8,128)} slice(f32[4,32,4,8192]{3,1,2,0:T(8,128)S(1)} %fusion.25), slice={[0:4], [0:32], [0:4], [1:8192]} | slice | bytes 33550336 | tf_op jit(solution)/shard_map/jit(_roll_static)/slice | solution.py:69
  217.6 1.9 copy-done.2
  219.4 9.9 %fusion.20 = f32[4,32,4,8192]{3,1,2,0:T(8,128)S(1)} fusion(bf16[4,3,32,32,1]{3,1,2,0,4:T(4,128)(2,1)S(1)} %bitcast.119, bf16[4,1,32,4,8192]{4,2,3,0,1:T(8,128)(2,1)} %get-tuple-element.12, bf16[4,1,32,4,8192]{4,2,3,0,1:T(8,128)(2,1)S(1)} %bitcast.109, bf16[4,1,32,4,8192]{4,2,3,0,1:T(8,128)(2,1)} %get-tuple-element.11), kind=kOutput, calls=%fused_computation.26 | convolution fusion | flops 830472192 | bytes 41967616 | tf_op jit(solution)/shard_map/otij,otjrw->oirw/dot_general | solution.py:68
  229.3 0.1 slice.190
  229.5 5.6 %copy-done.9 = f32[4,32,4,8192]{3,1,2,0:T(8,128)} copy-done((f32[4,32,4,8192]{3,1,2,0:T(8,128)}, f32[4,32,4,8192]{3,1,2,0:T(8,128)S(1)}, u32[]{:S(2)}) %copy-start.9) | copy-done | bytes 16777240
  235.1 20.1 %fusion.15 = bf16[4,32,4,8192]{3,1,2,0:T(8,128)(2,1)S(1)} fusion(f32[4,32,4,8191]{3,1,2,0:T(8,128)} %bitcast.124, f32[4,32,4,1]{3,1,2,0:T(8,128)S(1)} %slice.190, f32[4,32,4,1]{3,1,2,0:T(8,128)S(1)} %slice-done.6, f32[4,32,4,8191]{3,1,2,0:T(8,128)} %slice.192, f32[32]{0:T(128)S(1)} %get-tuple-element.20, bf16[4,3,32,32,1]{3,1,2,0,4:T(4,128)(2,1)S(1)} %bitcast.117, ...), kind=kOutput, calls=%fused_computation.18 | convolution fusion | flops 859832320 | bytes 67133568 | tf_op jit(solution)/shard_map/otij,otjrw->oirw/dot_general | solution.py:68
  255.2 0.0 copy-start
  255.2 0.3 fusion.114
  255.5 2.6 collective-permute-start.4
  258.1 0.2 collective-permute-start.5
  258.3 8.1 %fusion.85 = f32[4,4,8192,32]{2,3,1,0:T(8,128)} fusion(bf16[4,32,4,8192]{3,1,2,0:T(8,128)(2,1)S(1)} %fusion.15, bf16[2,3,32,32]{3,2,1,0:T(8,128)(2,1)S(1)} %copy-done.5), kind=kOutput, calls=%fused_computation.91 | convolution fusion | flops 268435456 | bytes 25174016 | tf_op jit(solution)/shard_map/ij,ojrw->oirw/dot_general | solution.py:50
  266.4 36.8 %collective-permute-done.4 = bf16[1,32,4,8192]{3,1,2,0:T(8,128)(2,1)S(1)} collective-permute-done((bf16[1,32,4,8192]{3,1,2,0:T(8,128)(2,1)S(1)}, bf16[1,32,4,8192]{3,1,2,0:T(8,128)(2,1)S(1)}, u32[]{:S(2)}, u32[]{:S(2)}) %collective-permute-start.4) | collective-permute-done | bytes 2097184 | tf_op jit(solution)/shard_map/ppermute | solution.py:22
  303.2 7.0 %fusion.40 = f32[4,4,8192,32]{2,3,1,0:T(8,128)} fusion(bf16[4,32,4,8192]{3,1,2,0:T(8,128)(2,1)S(1)} %fusion.15, bf16[1,32,4,8192]{3,1,2,0:T(8,128)(2,1)S(1)} %collective-permute-done.4, bf16[2,3,32,32]{3,2,1,0:T(8,128)(2,1)S(1)} %copy-done.5), kind=kOutput, calls=%fused_computation.38 | convolution fusion | flops 285212672 | bytes 27271168 | tf_op jit(solution)/shard_map/ij,ojrw->oirw/dot_general | solution.py:50
  310.1 0.0 collective-permute-done.5
  310.1 17.1 %add_convert_fusion = bf16[4,4,8192,32]{2,3,1,0:T(8,128)(2,1)} fusion(f32[4,4,8192,32]{2,3,1,0:T(8,128)} %fusion.40, f32[4,4,8192,32]{2,3,1,0:T(8,128)} %fusion.85, bf16[1,32,4,8192]{3,1,2,0:T(8,128)(2,1)S(1)} %collective-permute-done.5, bf16[4,32,4,8192]{3,1,2,0:T(8,128)(2,1)} %copy-done, bf16[2,3,32,32]{3,2,1,0:T(8,128)(2,1)S(1)} %copy-done.5), kind=kOutput, calls=%fused_computation.24 | convolution fusion | flops 297795584 | bytes 52436992 | tf_op jit(solution)/shard_map/ij,ojrw->oirw/dot_general | solution.py:50
  327.3 4.7 fusion.113
  332.0 2.5 collective-permute-start.6
  334.5 3.9 collective-permute-start.7
  338.4 0.6 convolution_convert_fusion.1
  339.1 0.4 slice.182
  339.5 0.4 slice.147
  339.8 0.4 slice.181
  340.2 83.0 %collective-permute-done.6 = bf16[4,32,1,8192]{3,1,2,0:T(8,128)(2,1)S(1)} collective-permute-done((bf16[4,32,1,8192]{3,1,2,0:T(8,128)(2,1)}, bf16[4,32,1,8192]{3,1,2,0:T(8,128)(2,1)S(1)}, u32[]{:S(2)}, u32[]{:S(2)}) %collective-permute-start.6) | collective-permute-done | bytes 2097184 | tf_op jit(solution)/shard_map/ppermute | solution.py:22
  423.2 3.3 collective-permute-done.7
  426.5 12.0 %fusion.37 = (bf16[4,1,32,4,8192]{4,2,3,0,1:T(8,128)(2,1)}, bf16[4,1,32,4,8192]{4,2,3,0,1:T(8,128)(2,1)}) fusion(bf16[4,32,4,8192]{3,1,2,0:T(8,128)(2,1)} %bitcast.111, bf16[4,32,1,8192]{3,1,2,0:T(8,128)(2,1)S(1)} %collective-permute-done.6, bf16[4,32,1,8192]{3,1,2,0:T(8,128)(2,1)} %collective-permute-done.7), kind=kLoop, calls=%fused_computation.33 | loop fusion | flops 8388608 | bytes 29360128 | tf_op jit(solution)/shard_map/stack | solution.py:61
  438.5 11.8 %fusion.33 = f32[4,32,4,8192]{3,1,2,0:T(8,128)S(1)} fusion(bf16[4,3,32,32,1]{3,1,2,0,4:T(4,128)(2,1)S(1)} %bitcast.122, bf16[4,1,32,4,8192]{4,2,3,0,1:T(8,128)(2,1)} %get-tuple-element.6, bf16[4,1,32,4,8192]{4,2,3,0,1:T(8,128)(2,1)} %bitcast.112, bf16[4,1,32,4,8192]{4,2,3,0,1:T(8,128)(2,1)} %get-tuple-element.5), kind=kOutput, calls=%fused_computation.29 | convolution fusion | flops 830472192 | bytes 41967616 | tf_op jit(solution)/shard_map/otij,otjrw->oirw/dot_general | solution.py:68
  450.3 9.0 %slice.200 = f32[4,32,4,8191]{3,1,2,0:T(8,128)} slice(f32[4,32,4,8192]{3,1,2,0:T(8,128)S(1)} %fusion.33), slice={[0:4], [0:32], [0:4], [1:8192]} | slice | bytes 33550336 | tf_op jit(solution)/shard_map/jit(_roll_static)/slice | solution.py:69
  459.4 1.8 copy-done.3
  461.2 9.9 %fusion.28 = f32[4,32,4,8192]{3,1,2,0:T(8,128)S(1)} fusion(bf16[4,3,32,32,1]{3,1,2,0,4:T(4,128)(2,1)S(1)} %bitcast.120, bf16[4,1,32,4,8192]{4,2,3,0,1:T(8,128)(2,1)} %get-tuple-element.6, bf16[4,1,32,4,8192]{4,2,3,0,1:T(8,128)(2,1)S(1)} %bitcast.115, bf16[4,1,32,4,8192]{4,2,3,0,1:T(8,128)(2,1)} %get-tuple-element.5), kind=kOutput, calls=%fused_computation.28 | convolution fusion | flops 830472192 | bytes 41967616 | tf_op jit(solution)/shard_map/otij,otjrw->oirw/dot_general | solution.py:68
  471.1 0.0 copy-start.8
  471.1 5.7 %copy-done.8 = f32[4,32,4,8192]{3,1,2,0:T(8,128)} copy-done((f32[4,32,4,8192]{3,1,2,0:T(8,128)}, f32[4,32,4,8192]{3,1,2,0:T(8,128)S(1)}, u32[]{:S(2)}) %copy-start.8) | copy-done | bytes 16777240
  476.8 0.1 slice.198
  477.0 21.3 %fusion.19 = bf16[4,32,4,8192]{3,1,2,0:T(8,128)(2,1)} fusion(f32[4,32,4,8191]{3,1,2,0:T(8,128)} %bitcast.123, f32[4,32,4,1]{3,1,2,0:T(8,128)S(1)} %slice.198, f32[4,32,4,1]{3,1,2,0:T(8,128)S(1)} %slice-done.7, f32[4,32,4,8191]{3,1,2,0:T(8,128)} %slice.200, f32[32]{0:T(128)S(1)} %copy-done.13, bf16[4,3,32,32,1]{3,1,2,0,4:T(4,128)(2,1)S(1)} %bitcast.118, ...), kind=kOutput, calls=%fused_computation.23 | convolution fusion | flops 859832320 | bytes 67133568 | tf_op jit(solution)/shard_map/otij,otjrw->oirw/dot_general | solution.py:68
  498.3 12.2 %copy.27 = bf16[4,32,4,8192]{3,2,1,0:T(4,128)(2,1)} copy(bf16[4,32,4,8192]{3,1,2,0:T(8,128)(2,1)} %fusion.19) | data formatting | bytes 16777216 | tf_op jit(solution)/shard_map/convert_element_type | solution.py:71
  (35 shorter events, 0.1 us)
Async XLA Ops:
  0.0 17.7 %copy-start.5 = (bf16[2,3,32,32]{3,2,1,0:T(8,128)(2,1)S(1)}, bf16[2,3,32,32]{3,2,1,0:T(8,128)(2,1)}, u32[]{:S(2)}) copy-start(bf16[2,3,32,32]{3,2,1,0:T(8,128)(2,1)} %param.8) | copy-start | bytes 36868
  11.4 6.3 %copy-start.1 = (bf16[4,32,4,8192]{3,2,1,0:T(4,128)(2,1)S(1)}, bf16[4,32,4,8192]{3,2,1,0:T(4,128)(2,1)}, u32[]{:S(2)}) copy-start(bf16[4,32,4,8192]{3,2,1,0:T(4,128)(2,1)} %param.7) | copy-start | bytes 25165828
  16.3 44.2 %collective-permute-start = (bf16[1,32,4,8192]{3,1,2,0:T(8,128)(2,1)}, bf16[1,32,4,8192]{3,1,2,0:T(8,128)(2,1)}, u32[]{:S(2)}, u32[]{:S(2)}) collective-permute-start(bf16[1,32,4,8192]{3,1,2,0:T(8,128)(2,1)} %get-tuple-element.16), channel_id=1, source_target_pairs={{0,1},{1,2},{2,3},{3,0},{4,5},{5,6},{6,7},{7,4},{8,9},{9,10},{10,1... | collective-permute-start | bytes 6291464 | tf_op jit(solution)/shard_map/ppermute | solution.py:22
  17.2 43.4 %slice-start = ((s8[8388608]{0:T(1024)(128)(4,1)}), s8[4194304]{0:T(1024)(128)(4,1)S(1)}, s32[]{:S(2)}) async-start(s8[8388608]{0:T(1024)(128)(4,1)} %bitcast.101), calls=%async_computation | async-start | bytes 8388608
  17.2 43.4 %slice-start.1 = ((s8[8388608]{0:T(1024)(128)(4,1)}), s8[4194304]{0:T(1024)(128)(4,1)S(1)}, s32[]{:S(2)}) async-start(s8[8388608]{0:T(1024)(128)(4,1)} %bitcast.101), calls=%async_computation.1 | async-start | bytes 8388608
  17.2 53.3 %collective-permute-start.1 = (bf16[1,32,4,8192]{3,1,2,0:T(8,128)(2,1)}, bf16[1,32,4,8192]{3,1,2,0:T(8,128)(2,1)S(1)}, u32[]{:S(2)}, u32[]{:S(2)}) collective-permute-start(bf16[1,32,4,8192]{3,1,2,0:T(8,128)(2,1)} %get-tuple-element.15), channel_id=1, source_target_pairs={{1,0},{2,1},{3,2},{0,3},{5,4},{6,5},{7,6},{4,7},{9,8},{10,9},{11,1... | collective-permute-start | bytes 6291464 | tf_op jit(solution)/shard_map/ppermute | solution.py:25
  87.5 11.0 %copy-start.11 = (f32[9]{0:T(128)S(1)}, f32[9]{0:T(128)}, u32[]{:S(2)}) copy-start(f32[9]{0:T(128)} %constant.38) | copy-start | bytes 112
  87.5 11.0 %copy-start.12 = (f32[9]{0:T(128)S(1)}, f32[9]{0:T(128)}, u32[]{:S(2)}) copy-start(f32[9]{0:T(128)} %constant.39) | copy-start | bytes 112
  87.5 11.1 %copy-start.4 = (bf16[2,9,32,32]{3,2,1,0:T(8,128)(2,1)S(1)}, bf16[2,9,32,32]{3,2,1,0:T(8,128)(2,1)}, u32[]{:S(2)}) copy-start(bf16[2,9,32,32]{3,2,1,0:T(8,128)(2,1)} %param.9) | copy-start | bytes 110596
  87.5 11.1 %copy-start.6 = (f32[9,9]{1,0:T(8,128)S(1)}, f32[9,9]{1,0:T(8,128)}, u32[]{:S(2)}) copy-start(f32[9,9]{1,0:T(8,128)} %constant.35.clone) | copy-start | bytes 976
  87.5 11.1 %copy-start.7 = (f32[9,9]{1,0:T(8,128)S(1)}, f32[9,9]{1,0:T(8,128)}, u32[]{:S(2)}) copy-start(f32[9,9]{1,0:T(8,128)} %constant.36.clone) | copy-start | bytes 976
  87.5 13.0 %copy-start.10 = (f32[2,32]{1,0:T(2,128)S(1)}, f32[2,32]{1,0:T(2,128)}, u32[]{:S(2)}) copy-start(f32[2,32]{1,0:T(2,128)} %param.10) | copy-start | bytes 772
  92.3 90.0 %collective-permute-start.2 = (bf16[4,32,1,8192]{3,1,2,0:T(8,128)(2,1)}, bf16[4,32,1,8192]{3,1,2,0:T(8,128)(2,1)S(1)}, u32[]{:S(2)}, u32[]{:S(2)}) collective-permute-start(bf16[4,32,1,8192]{3,1,2,0:T(8,128)(2,1)} %get-tuple-element.13), channel_id=1, source_target_pairs={{0,4},{4,8},{8,12},{12,16},{16,20},{20,24},{24,28},{1,5},{5,9},{9,... | collective-permute-start | bytes 6291464 | tf_op jit(solution)/shard_map/ppermute | solution.py:22
  95.4 92.4 %collective-permute-start.3 = (bf16[4,32,1,8192]{3,1,2,0:T(8,128)(2,1)}, bf16[4,32,1,8192]{3,1,2,0:T(8,128)(2,1)}, u32[]{:S(2)}, u32[]{:S(2)}) collective-permute-start(bf16[4,32,1,8192]{3,1,2,0:T(8,128)(2,1)} %get-tuple-element.14), channel_id=1, source_target_pairs={{4,0},{8,4},{12,8},{16,12},{20,16},{24,20},{28,24},{5,1},{9,5},{13... | collective-permute-start | bytes 6291464 | tf_op jit(solution)/shard_map/ppermute | solution.py:25
  100.5 98.2 %slice-start.2 = ((s8[8388608]{0:T(1024)(128)(4,1)}), s8[4194304]{0:T(1024)(128)(4,1)S(1)}, s32[]{:S(2)}) async-start(s8[8388608]{0:T(1024)(128)(4,1)} %bitcast.106), calls=%async_computation.2 | async-start | bytes 8388608
  101.0 97.7 %slice-start.3 = ((s8[8388608]{0:T(1024)(128)(4,1)}), s8[4194304]{0:T(1024)(128)(4,1)S(1)}, s32[]{:S(2)}) async-start(s8[8388608]{0:T(1024)(128)(4,1)} %bitcast.106), calls=%async_computation.3 | async-start | bytes 8388608
  208.5 10.9 %copy-start.2 = (f32[4,32,4,8192]{3,1,2,0:T(8,128)}, f32[4,32,4,8192]{3,1,2,0:T(8,128)S(1)}, u32[]{:S(2)}) copy-start(f32[4,32,4,8192]{3,1,2,0:T(8,128)S(1)} %fusion.25) | copy-start | bytes 50331652
  219.4 15.6 %slice-start.6 = ((f32[4,32,4,8192]{3,1,2,0:T(8,128)}), f32[4,32,4,1]{3,1,2,0:T(8,128)S(1)}, s32[]{:S(2)}) async-start(f32[4,32,4,8192]{3,1,2,0:T(8,128)} %copy-done.2), calls=%async_computation.6 | async-start | bytes 524288 | tf_op jit(solution)/shard_map/jit(_roll_static)/slice | solution.py:69
  229.3 5.8 %copy-start.9 = (f32[4,32,4,8192]{3,1,2,0:T(8,128)}, f32[4,32,4,8192]{3,1,2,0:T(8,128)S(1)}, u32[]{:S(2)}) copy-start(f32[4,32,4,8192]{3,1,2,0:T(8,128)S(1)} %fusion.20) | copy-start | bytes 50331652
  255.2 48.0 %copy-start = (bf16[4,32,4,8192]{3,1,2,0:T(8,128)(2,1)}, bf16[4,32,4,8192]{3,1,2,0:T(8,128)(2,1)S(1)}, u32[]{:S(2)}) copy-start(bf16[4,32,4,8192]{3,1,2,0:T(8,128)(2,1)S(1)} %fusion.15) | copy-start | bytes 25165828
  255.5 47.7 %collective-permute-start.4 = (bf16[1,32,4,8192]{3,1,2,0:T(8,128)(2,1)S(1)}, bf16[1,32,4,8192]{3,1,2,0:T(8,128)(2,1)S(1)}, u32[]{:S(2)}, u32[]{:S(2)}) collective-permute-start(bf16[1,32,4,8192]{3,1,2,0:T(8,128)(2,1)S(1)} %get-tuple-element.10), channel_id=1, source_target_pairs={{0,1},{1,2},{2,3},{3,0},{4,5},{5,6},{6,7},{7,4},{8,9},{9,10},{10,1... | collective-permute-start | bytes 6291464 | tf_op jit(solution)/shard_map/ppermute | solution.py:22
  258.1 52.0 %collective-permute-start.5 = (bf16[1,32,4,8192]{3,1,2,0:T(8,128)(2,1)S(1)}, bf16[1,32,4,8192]{3,1,2,0:T(8,128)(2,1)S(1)}, u32[]{:S(2)}, u32[]{:S(2)}) collective-permute-start(bf16[1,32,4,8192]{3,1,2,0:T(8,128)(2,1)S(1)} %get-tuple-element.9), channel_id=1, source_target_pairs={{1,0},{2,1},{3,2},{0,3},{5,4},{6,5},{7,6},{4,7},{9,8},{10,9},{11,1... | collective-permute-start | bytes 6291464 | tf_op jit(solution)/shard_map/ppermute | solution.py:25
  332.0 91.3 %collective-permute-start.6 = (bf16[4,32,1,8192]{3,1,2,0:T(8,128)(2,1)}, bf16[4,32,1,8192]{3,1,2,0:T(8,128)(2,1)S(1)}, u32[]{:S(2)}, u32[]{:S(2)}) collective-permute-start(bf16[4,32,1,8192]{3,1,2,0:T(8,128)(2,1)} %get-tuple-element.7), channel_id=1, source_target_pairs={{0,4},{4,8},{8,12},{12,16},{16,20},{20,24},{24,28},{1,5},{5,9},{9,... | collective-permute-start | bytes 6291464 | tf_op jit(solution)/shard_map/ppermute | solution.py:22
  334.5 92.0 %collective-permute-start.7 = (bf16[4,32,1,8192]{3,1,2,0:T(8,128)(2,1)}, bf16[4,32,1,8192]{3,1,2,0:T(8,128)(2,1)}, u32[]{:S(2)}, u32[]{:S(2)}) collective-permute-start(bf16[4,32,1,8192]{3,1,2,0:T(8,128)(2,1)} %get-tuple-element.8), channel_id=1, source_target_pairs={{4,0},{8,4},{12,8},{16,12},{20,16},{24,20},{28,24},{5,1},{9,5},{13... | collective-permute-start | bytes 6291464 | tf_op jit(solution)/shard_map/ppermute | solution.py:25
  426.5 34.7 %slice-start.4 = ((s8[8388608]{0:T(1024)(128)(4,1)}), s8[4194304]{0:T(1024)(128)(4,1)S(1)}, s32[]{:S(2)}) async-start(s8[8388608]{0:T(1024)(128)(4,1)} %bitcast.113), calls=%async_computation.4 | async-start | bytes 8388608
  438.5 22.6 %slice-start.5 = ((s8[8388608]{0:T(1024)(128)(4,1)}), s8[4194304]{0:T(1024)(128)(4,1)S(1)}, s32[]{:S(2)}) async-start(s8[8388608]{0:T(1024)(128)(4,1)} %bitcast.113), calls=%async_computation.5 | async-start | bytes 8388608
  450.3 10.9 %copy-start.3 = (f32[4,32,4,8192]{3,1,2,0:T(8,128)}, f32[4,32,4,8192]{3,1,2,0:T(8,128)S(1)}, u32[]{:S(2)}) copy-start(f32[4,32,4,8192]{3,1,2,0:T(8,128)S(1)} %fusion.33) | copy-start | bytes 50331652
  461.2 15.8 %slice-start.7 = ((f32[4,32,4,8192]{3,1,2,0:T(8,128)}), f32[4,32,4,1]{3,1,2,0:T(8,128)S(1)}, s32[]{:S(2)}) async-start(f32[4,32,4,8192]{3,1,2,0:T(8,128)} %copy-done.3), calls=%async_computation.7 | async-start | bytes 524288 | tf_op jit(solution)/shard_map/jit(_roll_static)/slice | solution.py:69
  461.2 15.8 %copy-start.13 = (f32[32]{0:T(128)S(1)}, f32[32]{0:T(128)}, u32[]{:S(2)}) copy-start(f32[32]{0:T(128)} %get-tuple-element.19) | copy-start | bytes 388
  471.1 5.7 %copy-start.8 = (f32[4,32,4,8192]{3,1,2,0:T(8,128)}, f32[4,32,4,8192]{3,1,2,0:T(8,128)S(1)}, u32[]{:S(2)}) copy-start(f32[4,32,4,8192]{3,1,2,0:T(8,128)S(1)} %fusion.28) | copy-start | bytes 50331652
where the time goes:
time: 516 us; the launch traced here: 511 us
  waiting for transfers between devices  235 us (46%)
  matrix products  161 us (31%)
  local copies, waits for them, and re-layouts  74.5 us (14%)
  other arithmetic  22.9 us (4%)
  starting transfers between devices  16.7 us (3%)
    ppermute x4, waiting for transfers between devices, extended_2(): lax.ppermute(lax.slice_in_dim(block, block.shape[dim] - width, None, axis...  226 us
    dot_general x6, matrix products, conv_layer(): jnp.einsum('otij,otjrw->oirw', taps, row_stack, preferred_element_type=jn...  82.8 us
    dot_general x6, matrix products, mix_orients(): jnp.einsum('ij,ojrw->oirw', mixing[offset], extended[offset:offset + coun...  76.6 us
    unnamed x41, local copies, waits for them, and re-layouts  26.5 us
    another operation x2, other arithmetic, conv_layer(): jnp.stack([padded[:, :, row_start:row_start + out_rows, :] for row_start...  22.8 us
    slice x8, local copies, waits for them, and re-layouts, conv_layer(): term = jnp.roll(term, -col_shift, axis=3)  18.4 us
    convert_element_type x1, local copies, waits for them, and re-layouts, conv_layer(): jax.nn.relu(running + bias_row[None, :, None, None]).astype(jnp.bfloat16)  12.2 us
  transfers between devices with their start and end apart: 8, of which 6 were waited for; matrix products, arithmetic and copies ran while one was open for 9% of the time, Pallas kernels for 0%

commit v1 on v0

v1 whole, which is shorter than its diff:
```python
import functools

import jax
import jax.numpy as jnp
import numpy as np
from jax import lax
from jax.experimental import pallas as pl
from jax.experimental.pallas import tpu as pltpu
from jax.sharding import PartitionSpec as P

LAYERS = 2
EDGE = 128
SHARES = (5, 7, 10, 10)
JOINED = ((0, 1), (2,), (3,))
COST = {"mix": 10**6, "conv": 10**11}
VMEM_BYTES = 20 * 2**20
BF16 = jnp.bfloat16
F32 = jnp.float32

CYCLE = (0, 1, 2, 5, 8, 7, 6, 3)

ANY = pl.BlockSpec(memory_space=pl.ANY)
HBM = pl.BlockSpec(memory_space=pltpu.HBM)
VMEM = pl.BlockSpec(memory_space=pltpu.VMEM)
SMEM = pl.BlockSpec(memory_space=pltpu.SMEM)


def tile_of(length, most):
    blocks = length // EDGE
    return EDGE * max(d for d in range(1, most // EDGE + 1) if blocks % d == 0)


def one_hot(shape, hit):
    first = lax.broadcasted_iota(jnp.int32, shape, 0)
    second = lax.broadcasted_iota(jnp.int32, shape, 1)
    return jnp.where(hit(first, second), 1.0, 0.0).astype(BF16)


def run_copies(copies, sems):
    started = [pltpu.make_async_copy(src, dst, sems.at[i]) for i, (src, dst) in enumerate(copies)]
    for copy in started:
        copy.start()
    for copy in started:
        copy.wait()


def call(body, outs, out_specs, in_specs, scratch, args, aliases=None, cost=1):
    return pl.pallas_call(
        body,
        out_shape=outs,
        in_specs=in_specs,
        out_specs=out_specs,
        scratch_shapes=scratch,
        input_output_aliases=aliases or {},
        cost_estimate=pl.CostEstimate(flops=cost, bytes_accessed=1, transcendentals=0),
        compiler_params=pltpu.CompilerParams(vmem_limit_bytes=VMEM_BYTES),
    )(*args)


def segments(start, stop, width):
    pieces, at = [], start
    while at < stop:
        begin = at % width
        length = min(stop - at, width - begin)
        pieces.append((begin, at - start, length))
        at += length
    return pieces


def mix_weight_body(channels, rows, mix_ref, *out_refs):
    span = channels * rows
    for layer in range(LAYERS):
        for offset in range(3):
            for row in range(rows):
                if layer == 0:
                    place = one_hot((channels, span), lambda c, k: k == c * rows + row)
                else:
                    place = one_hot((channels, span), lambda c, k: k == row * channels + c)
                block = jnp.dot(mix_ref[layer, offset], place, preferred_element_type=F32)
                out_refs[layer][pl.ds(row * channels, channels), pl.ds(offset * span, span)] = block.astype(BF16)


def conv_weight_body(count, channels, rows, first_ref, kernel_ref, *refs):
    out_refs = refs[-LAYERS:]
    span = channels * rows
    depth = channels * (rows + 2)
    swap = one_hot((span, span), lambda a, b: b == (a % rows) * channels + a // rows)
    for here in range(count):
        orient = first_ref[0] + here
        weights = []
        for diff in range(8):
            halves = jnp.bitwise_and(2 * diff - orient + 8, 15) - 8
            weights.append(jnp.maximum(2 - jnp.abs(halves), 0).astype(F32) * 0.5)
        for layer in range(LAYERS):
            taps = [kernel_ref[layer, tap].astype(F32) for tap in range(9)]
            turned = [None] * 9
            turned[4] = taps[4]
            for a in range(8):
                total = None
                for diff in range(8):
                    term = weights[diff] * taps[CYCLE[(a - diff) % 8]]
                    total = term if total is None else total + term
                turned[CYCLE[a]] = total
            turned = jnp.concatenate(turned, axis=0).astype(BF16)
            spread = [
                jnp.dot(
                    turned,
                    one_hot((channels, depth), lambda c, k: k == line * channels + c),
                    preferred_element_type=F32,
                )
                for line in range(rows + 2)
            ]
            for col in range(3):
                blocks = []
                for row in range(rows):
                    total = None
                    for dy in range(3):
                        tap = 3 * dy + col
                        term = spread[row + dy][tap * channels : (tap + 1) * channels]
                        total = term if total is None else total + term
                    blocks.append(total)
                block = jnp.concatenate(blocks, axis=0).astype(BF16)
                if layer == LAYERS - 1:
                    block = jnp.dot(swap, block, preferred_element_type=F32).astype(BF16)
                out_refs[layer][here, pl.ds(col * span, span), :] = block


def edge_copies(pieces, cur_ref, last_ref, first_ref):
    count = cur_ref.shape[0]
    copies = []
    for src, dst, size in pieces:
        source, target = pl.ds(src, size), pl.ds(dst, size)
        copies.append((cur_ref.at[count - 1, ..., source], last_ref.at[..., target]))
        copies.append((cur_ref.at[0, ..., source], first_ref.at[..., target]))
    return copies


def pick_body(pieces, n_deps, cur_ref, *refs):
    last_ref, first_ref, sems = refs[n_deps:]
    run_copies(edge_copies(pieces, cur_ref, last_ref, first_ref), sems)


def mix_body(count, channels, rows, pieces, next_pieces, n_deps, *refs):
    weight_ref, cur_ref, low_ref, high_ref = refs[:4]
    refs = refs[4:]
    if next_pieces:
        next_ref, refs = refs[0], refs[1:]
    refs = refs[n_deps:]
    main_ref, top_ref, bottom_ref = refs[:3]
    refs = refs[3:]
    span = channels * rows
    length = main_ref.shape[-1]
    copies = []
    if next_pieces:
        send_ref, last_ref, first_ref = next_ref, *refs[:2]
        refs = refs[2:]
        copies += edge_copies(next_pieces, send_ref, last_ref, first_ref)
    if pieces is None:
        flat, sems = refs
        copies.append((cur_ref, flat.at[pl.ds(1, count)]))
        copies.append((low_ref, flat.at[0]))
        copies.append((high_ref, flat.at[count + 1]))
    else:
        flat, raw, sems = refs
        for src, dst, size in pieces:
            copies.append((cur_ref.at[:, :, :, pl.ds(src, size)], raw.at[pl.ds(1, count), :, :, pl.ds(dst, size)]))
        copies.append((low_ref, raw.at[0]))
        copies.append((high_ref, raw.at[count + 1]))
    run_copies(copies, sems)
    step = tile_of(length, 1408)

    @pl.loop(0, length // step)
    def _(index):
        cols = pl.ds(pl.multiple_of(index * step, EDGE), step)
        if pieces is not None:
            for slot in range(count + 2):
                flat[slot, :, cols] = raw[slot, :, :, cols].reshape(span, step)
        for here in range(count):
            stack = flat[pl.ds(here, 3), :, cols].reshape(3 * span, step)
            mixed = jnp.dot(weight_ref[...], stack, preferred_element_type=F32).astype(BF16)
            main_ref[here, :, cols] = mixed
            top_ref[here, :, cols] = mixed[:channels]
            bottom_ref[here, :, cols] = mixed[span - channels :]


def conv_body(count, channels, rows, cuts, n_arrays, n_deps, place, *refs):
    weight_ref, bias_ref = refs[:2]
    pieces = refs[2 : 2 + 3 * n_arrays]
    refs = refs[2 + 3 * n_arrays + n_deps :]
    span = channels * rows
    if place is None:
        main_ref, held, sems = refs
    else:
        out_ref, done, held, sems = refs
    length = held.shape[-1] - 2 * EDGE
    copies = []
    for array, src, dst, size in cuts:
        main, top, bottom = pieces[3 * array : 3 * array + 3]
        source, target = pl.ds(src, size), pl.ds(dst, size)
        copies.append((top.at[:, :, source], held.at[:, pl.ds(0, channels), target]))
        copies.append((main.at[:, :, source], held.at[:, pl.ds(channels, span), target]))
        copies.append((bottom.at[:, :, source], held.at[:, pl.ds(channels + span, channels), target]))
    run_copies(copies, sems)
    step = tile_of(length, 1664)

    @pl.loop(0, length // step)
    def _(index):
        begin = pl.multiple_of(index * step, EDGE)
        cols = pl.ds(begin, step)
        for here in range(count):
            block = held[here, :, pl.ds(begin, step + 2 * EDGE)]
            terms = jnp.dot(weight_ref[here], block, preferred_element_type=F32)
            total = (
                pltpu.roll(terms[:span], 1, 1)
                + terms[span : 2 * span]
                + pltpu.roll(terms[2 * span :], step + 2 * EDGE - 1, 1)
            )
            total = jnp.maximum(total[:, EDGE : EDGE + step] + bias_ref[...], 0.0).astype(BF16)
            if place is None:
                main_ref[here, :, cols] = total
            else:
                done[here, :, :, cols] = total.reshape(channels, rows, step)

    if place is not None:
        run_copies([(done, out_ref.at[:, :, :, pl.ds(place, length)])], sems)


def ring(axis, count, periodic):
    forward = [(i, i + 1) for i in range(count - 1)]
    if periodic:
        forward.append((count - 1, 0))
    return (
        lambda block: lax.ppermute(block, axis, forward),
        lambda block: lax.ppermute(block, axis, [(b, a) for a, b in forward]),
    )


def local(sizes, features, mix_weights, kernels, bias_terms):
    count, channels, rows, width = features.shape
    span = channels * rows
    features = pltpu.with_memory_space_constraint(features, pltpu.HBM)
    orient_up, orient_down = ring("orient", sizes["orient"], True)
    lat_up, lat_down = ring("lat", sizes["lat"], False)
    n = len(SHARES)
    shape = jax.ShapeDtypeStruct
    dma = pltpu.SemaphoreType.DMA

    bounds = [-2 * EDGE]
    for share in SHARES:
        bounds.append(bounds[-1] + share * (width // sum(SHARES)))
    ranges = [[(bounds[i], bounds[i + 1]) for i in range(n)]]
    joined = [(bounds[group[0]], bounds[group[-1] + 1]) for group in JOINED]
    for _ in range(LAYERS):
        joined = [(a - EDGE, b - EDGE) for a, b in joined]
        joined[0] = (joined[0][0] + 2 * EDGE, joined[0][1])
        joined[-1] = (joined[-1][0], joined[-1][1] + 2 * EDGE)
        ranges.append(joined)

    first_orient = (lax.axis_index("orient") * count).astype(jnp.int32).reshape(1)
    bias_rows = jnp.tile(bias_terms[: LAYERS - 1], (1, rows))
    bias_last = jnp.repeat(bias_terms[LAYERS - 1 :], rows, axis=1)
    biases = [row[:, None] for row in (*bias_rows, *bias_last)]

    mix_all = call(
        functools.partial(mix_weight_body, channels, rows),
        (shape((span, 3 * span), BF16),) * LAYERS,
        (VMEM,) * LAYERS,
        [VMEM],
        [],
        [mix_weights],
    )

    def edges(layer, index):
        a, b = ranges[layer][index]
        if layer == 0:
            return segments(a, b, width), shape((channels, rows, b - a), BF16)
        return [(0, 0, b - a)], shape((span, b - a), BF16)

    def mix(layer, index, cur, low, high, following, deps):
        a, b = ranges[layer][index]
        length = b - a
        pieces = next_pieces = None
        outs = [shape((count, span, length), BF16)] + [shape((count, channels, length), BF16)] * 2
        specs = [VMEM, VMEM, VMEM]
        scratch = [pltpu.VMEM((count + 2, span, length), BF16)]
        copies = 3
        args = [mix_all[layer], cur, low, high]
        if layer == 0:
            pieces = segments(a, b, width)
            copies = 2 + len(pieces)
            scratch.append(pltpu.VMEM((count + 2, channels, rows, length), BF16))
        if following is not None:
            source, next_layer, next_index = following
            args.append(source)
            next_pieces, block = edges(next_layer, next_index)
            copies += 2 * len(next_pieces)
            outs += [block] * 2
            specs += [VMEM, VMEM]
        scratch.append(dma((copies,)))
        return call(
            functools.partial(mix_body, count, channels, rows, pieces, next_pieces, len(deps)),
            tuple(outs),
            tuple(specs),
            [VMEM] + [ANY] * (len(args) - 1 + len(deps)),
            scratch,
            [*args, *deps],
            cost=COST["mix"],
        )

    def conv(layer, index, weights, held, out=None, deps=()):
        start, stop = ranges[layer + 1][index]
        need = (start - EDGE, stop + EDGE)
        used, cuts = [], []
        for which, (a, b) in enumerate(ranges[layer]):
            for turn in (0, width):
                lo, hi = max(need[0], a + turn), min(need[1], b + turn)
                if lo < hi:
                    if which not in used:
                        used.append(which)
                    cuts.append((used.index(which), lo - a - turn, lo - need[0], hi - lo))
        arrays = [array for which in used for array in held[which]]
        length = stop - start
        scratch = [
            pltpu.VMEM((count, span + 2 * channels, length + 2 * EDGE), BF16),
            dma((3 * len(cuts),)),
        ]
        aliases = {}
        deps = list(deps)
        if layer < LAYERS - 1:
            place = None
            outs = shape((count, span, length), BF16)
            specs = VMEM
        else:
            place = start
            outs = shape(features.shape, BF16)
            specs = ANY
            scratch.insert(0, pltpu.VMEM((count, channels, rows, length), BF16))
            if out is not None:
                aliases = {2 + len(arrays): 0}
                deps = [out] + deps
        return call(
            functools.partial(conv_body, count, channels, rows, cuts, len(used), len(deps), place),
            outs,
            specs,
            [VMEM, VMEM] + [ANY] * (len(arrays) + len(deps)),
            scratch,
            [weights[layer], biases[layer], *arrays, *deps],
            aliases,
            cost=COST["conv"],
        )

    stages = [(layer, index) for layer in range(LAYERS) for index in range(len(ranges[layer]))]
    current = {(0, index): features for index in range(n)}
    held = [[None] * len(ranges[layer]) for layer in range(LAYERS)]

    def pick(index, deps):
        pieces, block = edges(0, index)
        return call(
            functools.partial(pick_body, pieces, len(deps)),
            (block, block),
            (VMEM, VMEM),
            [ANY] * (1 + len(deps)),
            [dma((2 * len(pieces),))],
            [features, *deps],
        )

    def gate(pair, deps):
        return call(
            lambda *refs: None,
            tuple(shape(block.shape, BF16) for block in pair),
            (ANY, ANY),
            [ANY] * (2 + len(deps)),
            [],
            [*pair, *deps],
            {0: 0, 1: 1},
        )

    def send(pair):
        return orient_up(pair[0]), orient_down(pair[1])

    sent = pick(0, ())
    arrived = [send(sent)]
    second = pick(1, (*sent, *mix_all, *biases))
    arrived.append(send(gate(second, arrived[0])))
    weights = out = None
    token = ()
    finished = {group[-1]: index for index, group in enumerate(JOINED)}

    for stage in range(len(stages) + 1):
        if stage < len(stages):
            layer, index = stages[stage]
            low, high = arrived[stage]
            following = None
            if 1 <= stage < len(stages) - 1:
                following = (current[stages[stage + 1]], *stages[stage + 1])
            got = mix(layer, index, current[layer, index], low, high, following, token)
            edge_rows = got[1:3]
            if stage == 1:
                edge_rows = gate(edge_rows, held[0][0][1:])
            held[layer][index] = (got[0], lat_up(edge_rows[1]), lat_down(edge_rows[0]))
            if following is not None:
                arrived.append(send(got[3:]))
            token = (edge_rows[0],)
        if stage == 0:
            continue
        layer, index = stages[stage - 1]
        if layer == 0 and index not in finished:
            if weights is None:
                deps = token
                weights = call(
                    functools.partial(conv_weight_body, count, channels, rows),
                    (shape((count, 3 * span, span + 2 * channels), BF16),) * LAYERS,
                    (VMEM,) * LAYERS,
                    [SMEM, VMEM] + [ANY] * len(deps),
                    [],
                    [first_orient, kernels, *deps],
                    cost=COST["conv"],
                )
                token = (weights[0],)
        elif layer == 0:
            got = conv(layer, finished[index], weights, held[layer], out, token)
            current[layer + 1, finished[index]] = got
            token = (got,)
        else:
            out = conv(layer, index, weights, held[layer], out, token)
            token = ()
    return out


def solution(mesh):
    spec = P("orient", None, "lat", None)
    return jax.shard_map(
        functools.partial(local, dict(mesh.shape)),
        mesh=mesh,
        in_specs=(spec, P(), P(), P()),
        out_specs=spec,
        check_vma=False,
    )
```

time: 516 us -> 215 us (0.42)
  matrix products: 161 us -> 0 us
  waiting for transfers between devices: 235 us -> 102 us
  local copies, waits for them, and re-layouts: 74.5 us -> 1.34 us
  Pallas kernels: 0 us -> 61.2 us
  starting transfers between devices: 16.7 us -> 48.7 us
  other arithmetic: 22.9 us -> 0 us
    dot_general x14 -> x0, matrix products: 161 us -> none  [the longest x6 82.8 us: conv_layer(): jnp.einsum('otij,otjrw->oirw', taps, row_stack, preferred_element_type=jn...]
    ppermute x8 -> x28, waiting for transfers between devices: 235 us -> 102 us  [the longest x14 59.9 us: ring(): lax.ppermute(block, axis, [(b, a) for a, b in forward])]
    pallas_call x0 -> x19, Pallas kernels: none -> 61.2 us  [call(): pl.pallas_call(body, out_shape=outs, in_specs=in_specs, out_specs=out_spe...]
    slice x19 -> x1, local copies, waits for them, and re-layouts: 35.4 us -> 0.01 us  [local(): bias_last = jnp.repeat(bias_terms[LAYERS - 1:], rows, axis=1)]
    ppermute x8 -> x28, starting transfers between devices: 16.7 us -> 48.7 us  [the longest x14 27.7 us: ring(): lax.ppermute(block, axis, [(b, a) for a, b in forward])]
    unnamed x41 -> x14, local copies, waits for them, and re-layouts: 26.5 us -> 1.08 us
    another operation x2 -> x0, other arithmetic: 22.8 us -> none  [conv_layer(): jnp.stack([padded[:, :, row_start:row_start + out_rows, :] for row_start...]
    convert_element_type x1 -> x0, local copies, waits for them, and re-layouts: 12.2 us -> none  [conv_layer(): jax.nn.relu(running + bias_row[None, :, None, None]).astype(jnp.bfloat16)]
  transfers between devices with their start and end apart: 8 -> 28, of which waited for: 6 -> 16; matrix products, arithmetic and copies ran while one was open for 9% -> 0% of each run, Pallas kernels for 0% -> 25%
where the time goes in v1:
time: 215 us; the launch traced here: 214 us
  waiting for transfers between devices  102 us (47%)
  Pallas kernels  61.2 us (28%)
  starting transfers between devices  48.7 us (23%)
    pallas_call x19, Pallas kernels, call(): pl.pallas_call(body, out_shape=outs, in_specs=in_specs, out_specs=out_spe...  61.2 us
    ppermute x14, waiting for transfers between devices, ring(): lax.ppermute(block, axis, [(b, a) for a, b in forward])  59.9 us
    ppermute x14, waiting for transfers between devices, ring(): lax.ppermute(block, axis, forward)  42 us
    ppermute x14, starting transfers between devices, ring(): lax.ppermute(block, axis, [(b, a) for a, b in forward])  27.7 us
    ppermute x14, starting transfers between devices, ring(): lax.ppermute(block, axis, forward)  20.9 us
  transfers between devices with their start and end apart: 28, of which 16 were waited for; matrix products, arithmetic and copies ran while one was open for 0% of the time, Pallas kernels for 25%

profile of v1, /device:TPU:19, one launch (start us, length us, event | category | flops | bytes accessed | tf_op | source)
XLA Modules:
  0.0 213.8 jit_solution(4134685685279184319)
XLA Ops:
  0.0 1.1 shard_map.47
  1.2 0.9 collective-permute-start
  2.0 0.0 collective-permute-start.1
  2.0 0.2 shard_map.46
  2.3 0.1 broadcast_in_dim.5
  2.3 0.1 broadcast_in_dim.7.refs_5_.refs_1_
  2.4 0.1 tile.13.refs_4_.refs_1_
  2.5 1.2 shard_map.48
  3.7 4.0 %collective-permute-done.refs_2_ = bf16[32,4,1280]{2,1,0:T(4,128)(2,1)S(1)} collective-permute-done((bf16[32,4,1280]{2,1,0:T(4,128)(2,1)S(1)}, bf16[32,4,1280]{2,1,0:T(4,128)(2,1)S(1)}, u32[]{:S(2)}, u32[]{:S(2)}) %collective-permute-start) | collective-permute-done | bytes 327712 | tf_op jit(solution)/shard_map/ppermute | solution.py:233
  7.7 3.5 %collective-permute-done.1.refs_3_ = bf16[32,4,1280]{2,1,0:T(4,128)(2,1)S(1)} collective-permute-done((bf16[32,4,1280]{2,1,0:T(4,128)(2,1)S(1)}, bf16[32,4,1280]{2,1,0:T(4,128)(2,1)S(1)}, u32[]{:S(2)}, u32[]{:S(2)}) %collective-permute-start.1) | collective-permute-done | bytes 327712 | tf_op jit(solution)/shard_map/ppermute | solution.py:234
  11.2 0.5 collective-permute-start.3
  11.7 2.3 %shard_map.50 = (bf16[4,128,1280]{2,1,0:T(8,128)(2,1)S(1)}, bf16[4,32,1280]{2,1,0:T(8,128)(2,1)S(1)}, bf16[4,32,1280]{2,1,0:T(8,128)(2,1)S(1)}) custom-call(bf16[128,384]{1,0:T(8,128)(2,1)S(1)} %get-tuple-element.48.refs_2_.refs_0_, bf16[4,32,4,8192]{3,2,1,0:T(4,128)(2,1)} %refs_1_.7, bf16[32,4,1280]{2,1,0:T(4,128)(2,1)S(1)} %collective-permute-done.refs_2_, ...), custom_call_target="tpu_custom_call" | custom-call | flops 1000000 | bytes 1 | tf_op jit(solution)/shard_map/pallas_call | solution.py:48
  14.0 0.0 copy-start.3
  14.0 1.0 copy-done.3
  15.1 3.0 %collective-permute-start.5 = (bf16[4,32,1280]{2,1,0:T(8,128)(2,1)S(1)}, bf16[4,32,1280]{2,1,0:T(8,128)(2,1)S(1)}, u32[]{:S(2)}, u32[]{:S(2)}) collective-permute-start(bf16[4,32,1280]{2,1,0:T(8,128)(2,1)S(1)} %get-tuple-element.56.refs_5_), channel_id=1, source_target_pairs={{4,0},{8,4},{12,8},{16,12},{20,16},{24,20},{28,24},{5,1},{9,5},{13... | collective-permute-start | bytes 983048 | tf_op jit(solution)/shard_map/ppermute | solution.py:234
  18.1 2.3 %collective-permute-start.4 = (bf16[4,32,1280]{2,1,0:T(8,128)(2,1)S(1)}, bf16[4,32,1280]{2,1,0:T(8,128)(2,1)S(1)}, u32[]{:S(2)}, u32[]{:S(2)}) collective-permute-start(bf16[4,32,1280]{2,1,0:T(8,128)(2,1)S(1)} %get-tuple-element.59), channel_id=1, source_target_pairs={{0,4},{4,8},{8,12},{12,16},{16,20},{20,24},{24,28},{1,5},{5,9},{9,... | collective-permute-start | bytes 983048 | tf_op jit(solution)/shard_map/ppermute | solution.py:233
  20.3 0.0 copy-start.5
  20.4 3.2 %collective-permute-done.3.refs_3_ = bf16[32,4,1792]{2,1,0:T(4,128)(2,1)S(1)} collective-permute-done((bf16[32,4,1792]{2,1,0:T(4,128)(2,1)S(1)}, bf16[32,4,1792]{2,1,0:T(4,128)(2,1)S(1)}, u32[]{:S(2)}, u32[]{:S(2)}) %collective-permute-start.3) | collective-permute-done | bytes 458784 | tf_op jit(solution)/shard_map/ppermute | solution.py:234
  23.5 3.6 %shard_map.51 = (bf16[4,128,1792]{2,1,0:T(8,128)(2,1)S(1)}, bf16[4,32,1792]{2,1,0:T(8,128)(2,1)S(1)}, bf16[4,32,1792]{2,1,0:T(8,128)(2,1)S(1)}, bf16[32,4,2560]{2,1,0:T(4,128)(2,1)S(1)}, bf16[32,4,2560]{2,1,0:T(4,128)(2,1)S(1)}) custom-call(bf16[128,384]{1,0:T(8,128)(2,1)S(1)} %get-tuple-element.48.refs_2_.refs_0_, bf16[4,32,4,8192]{3,2,1,0:T(4,128)(2,1)} %refs_1_.7, ...), custom_call_target="tpu_custom_call" | custom-call | flops 1000000 | bytes 1 | tf_op jit(solution)/shard_map/pallas_call | solution.py:48
  27.1 0.1 collective-permute-start.8
  27.2 0.5 collective-permute-start.9
  27.7 4.3 %collective-permute-done.5.refs_3_.refs_4_ = bf16[4,32,1280]{2,1,0:T(8,128)(2,1)S(1)} collective-permute-done((bf16[4,32,1280]{2,1,0:T(8,128)(2,1)S(1)}, bf16[4,32,1280]{2,1,0:T(8,128)(2,1)S(1)}, u32[]{:S(2)}, u32[]{:S(2)}) %collective-permute-start.5) | collective-permute-done | bytes 327712 | tf_op jit(solution)/shard_map/ppermute | solution.py:234
  32.0 1.5 collective-permute-done.4.refs_2_.refs_3_
  33.5 4.1 %collective-permute-start.6 = (bf16[4,32,1792]{2,1,0:T(8,128)(2,1)S(1)}, bf16[4,32,1792]{2,1,0:T(8,128)(2,1)S(1)}, u32[]{:S(2)}, u32[]{:S(2)}) collective-permute-start(bf16[4,32,1792]{2,1,0:T(8,128)(2,1)S(1)} %get-tuple-element.65), channel_id=1, source_target_pairs={{0,4},{4,8},{8,12},{12,16},{16,20},{20,24},{24,28},{1,5},{5,9},{9,... | collective-permute-start | bytes 1376264 | tf_op jit(solution)/shard_map/ppermute | solution.py:233
  37.6 2.1 collective-permute-start.7
  39.7 2.2 %shard_map.53 = (bf16[4,384,192]{2,1,0:T(8,128)(2,1)S(1)}, bf16[4,384,192]{2,1,0:T(8,128)(2,1)S(1)}) custom-call(s32[1]{0:T(128)} %bitcast.first_ref, bf16[2,9,32,32]{3,2,1,0:T(8,128)(2,1)S(1)} %copy-done.5, bf16[4,32,1792]{2,1,0:T(8,128)(2,1)S(1)} %get-tuple-element.60.refs_0_), custom_call_target="tpu_custom_call" | custom-call | flops 99999997952 | bytes 1 | tf_op jit(solution)/shard_map/pallas_call | solution.py:48
  41.9 1.5 collective-permute-done.9.refs_3_
  43.4 4.2 %shard_map.54 = (bf16[4,128,2560]{2,1,0:T(8,128)(2,1)S(1)}, bf16[4,32,2560]{2,1,0:T(8,128)(2,1)S(1)}, bf16[4,32,2560]{2,1,0:T(8,128)(2,1)S(1)}, bf16[32,4,2560]{2,1,0:T(4,128)(2,1)S(1)}, bf16[32,4,2560]{2,1,0:T(4,128)(2,1)S(1)}) custom-call(bf16[128,384]{1,0:T(8,128)(2,1)S(1)} %get-tuple-element.48.refs_2_.refs_0_, bf16[4,32,4,8192]{3,2,1,0:T(4,128)(2,1)} %refs_1_.7, ...), custom_call_target="tpu_custom_call" | custom-call | flops 1000000 | bytes 1 | tf_op jit(solution)/shard_map/pallas_call | solution.py:48
  47.7 0.3 collective-permute-start.10
  48.0 0.2 collective-permute-start.11
  48.2 3.1 %collective-permute-start.14 = (bf16[4,32,2560]{2,1,0:T(8,128)(2,1)S(1)}, bf16[4,32,2560]{2,1,0:T(8,128)(2,1)S(1)}, u32[]{:S(2)}, u32[]{:S(2)}) collective-permute-start(bf16[4,32,2560]{2,1,0:T(8,128)(2,1)S(1)} %get-tuple-element.74), channel_id=1, source_target_pairs={{0,4},{4,8},{8,12},{12,16},{16,20},{20,24},{24,28},{1,5},{5,9},{9,... | collective-permute-start | bytes 1966088 | tf_op jit(solution)/shard_map/ppermute | solution.py:233
  51.4 5.5 %collective-permute-done.6.refs_6_.refs_3_ = bf16[4,32,1792]{2,1,0:T(8,128)(2,1)S(1)} collective-permute-done((bf16[4,32,1792]{2,1,0:T(8,128)(2,1)S(1)}, bf16[4,32,1792]{2,1,0:T(8,128)(2,1)S(1)}, u32[]{:S(2)}, u32[]{:S(2)}) %collective-permute-start.6) | collective-permute-done | bytes 458784 | tf_op jit(solution)/shard_map/ppermute | solution.py:233
  56.8 4.0 %collective-permute-start.15 = (bf16[4,32,2560]{2,1,0:T(8,128)(2,1)S(1)}, bf16[4,32,2560]{2,1,0:T(8,128)(2,1)S(1)}, u32[]{:S(2)}, u32[]{:S(2)}) collective-permute-start(bf16[4,32,2560]{2,1,0:T(8,128)(2,1)S(1)} %get-tuple-element.68.refs_8_), channel_id=1, source_target_pairs={{4,0},{8,4},{12,8},{16,12},{20,16},{24,20},{28,24},{5,1},{9,5},{13... | collective-permute-start | bytes 1966088 | tf_op jit(solution)/shard_map/ppermute | solution.py:234
  60.8 11.8 %collective-permute-done.7.refs_7_.refs_4_ = bf16[4,32,1792]{2,1,0:T(8,128)(2,1)S(1)} collective-permute-done((bf16[4,32,1792]{2,1,0:T(8,128)(2,1)S(1)}, bf16[4,32,1792]{2,1,0:T(8,128)(2,1)S(1)}, u32[]{:S(2)}, u32[]{:S(2)}) %collective-permute-start.7) | collective-permute-done | bytes 458784 | tf_op jit(solution)/shard_map/ppermute | solution.py:234
  72.6 5.0 %shard_map.55.refs_4_.refs_5_.refs_1_ = bf16[4,128,2816]{2,1,0:T(8,128)(2,1)S(1)} custom-call(bf16[4,384,192]{2,1,0:T(8,128)(2,1)S(1)} %get-tuple-element.62.refs_5_.refs_0_, f32[128,1]{1,0:T(8,128)S(1)} %tile.13.refs_4_.refs_1_, bf16[4,128,1280]{2,1,0:T(8,128)(2,1)S(1)} %copy-done.4, bf16[4,32,1280]{2,1,0:T(8,128)(2,1)S(1)} %collective-permute-done.4.refs_2_.refs_3_, ...), custom_call_target="tpu_custom_call" | custom-call | flops 99999997952 | bytes 1 | tf_op jit(solution)/shard_map/pallas_call | solution.py:48
  77.7 4.3 %shard_map.56 = (bf16[4,128,2560]{2,1,0:T(8,128)(2,1)S(1)}, bf16[4,32,2560]{2,1,0:T(8,128)(2,1)S(1)}, bf16[4,32,2560]{2,1,0:T(8,128)(2,1)S(1)}, bf16[128,2816]{1,0:T(8,128)(2,1)S(1)}, bf16[128,2816]{1,0:T(8,128)(2,1)S(1)}) custom-call(bf16[128,384]{1,0:T(8,128)(2,1)S(1)} %get-tuple-element.48.refs_2_.refs_0_, bf16[4,32,4,8192]{3,2,1,0:T(4,128)(2,1)} %refs_1_.7, ...), custom_call_target="tpu_custom_call" | custom-call | flops 1000000 | bytes 1 | tf_op jit(solution)/shard_map/pallas_call | solution.py:48
  82.0 1.3 collective-permute-start.12
  83.2 1.9 collective-permute-start.20
  85.2 4.4 %collective-permute-start.21 = (bf16[4,32,2560]{2,1,0:T(8,128)(2,1)S(1)}, bf16[4,32,2560]{2,1,0:T(8,128)(2,1)S(1)}, u32[]{:S(2)}, u32[]{:S(2)}) collective-permute-start(bf16[4,32,2560]{2,1,0:T(8,128)(2,1)S(1)} %get-tuple-element.75.refs_8_), channel_id=1, source_target_pairs={{4,0},{8,4},{12,8},{16,12},{20,16},{24,20},{28,24},{5,1},{9,5},{13... | collective-permute-start | bytes 1966088 | tf_op jit(solution)/shard_map/ppermute | solution.py:234
  89.6 4.4 %shard_map.57.refs_4_.refs_5_.refs_1_ = bf16[4,128,2560]{2,1,0:T(8,128)(2,1)S(1)} custom-call(bf16[4,384,192]{2,1,0:T(8,128)(2,1)S(1)} %get-tuple-element.62.refs_5_.refs_0_, f32[128,1]{1,0:T(8,128)S(1)} %tile.13.refs_4_.refs_1_, bf16[4,128,1792]{2,1,0:T(8,128)(2,1)S(1)} %get-tuple-element.64.refs_5_.refs_2_, ...), custom_call_target="tpu_custom_call" | custom-call | flops 99999997952 | bytes 1 | tf_op jit(solution)/shard_map/pallas_call | solution.py:48
  94.0 3.8 %collective-permute-done.12.refs_2_ = bf16[128,2816]{1,0:T(8,128)(2,1)S(1)} collective-permute-done((bf16[128,2816]{1,0:T(8,128)(2,1)S(1)}, bf16[128,2816]{1,0:T(8,128)(2,1)S(1)}, u32[]{:S(2)}, u32[]{:S(2)}) %collective-permute-start.12) | collective-permute-done | bytes 720928 | tf_op jit(solution)/shard_map/ppermute | solution.py:233
  97.8 2.8 %collective-permute-done.13.refs_3_ = bf16[128,2816]{1,0:T(8,128)(2,1)S(1)} collective-permute-done((bf16[128,2816]{1,0:T(8,128)(2,1)S(1)}, bf16[128,2816]{1,0:T(8,128)(2,1)S(1)}, u32[]{:S(2)}, u32[]{:S(2)}) %collective-permute-start.13) | collective-permute-done | bytes 720928 | tf_op jit(solution)/shard_map/ppermute | solution.py:234
  100.6 3.2 %shard_map.58 = (bf16[4,128,2816]{2,1,0:T(8,128)(2,1)S(1)}, bf16[4,32,2816]{2,1,0:T(8,128)(2,1)S(1)}, bf16[4,32,2816]{2,1,0:T(8,128)(2,1)S(1)}, bf16[128,2560]{1,0:T(8,128)(2,1)S(1)}, bf16[128,2560]{1,0:T(8,128)(2,1)S(1)}) custom-call(bf16[128,384]{1,0:T(8,128)(2,1)S(1)} %get-tuple-element.51.refs_3_.refs_0_, ...), custom_call_target="tpu_custom_call" | custom-call | flops 1000000 | bytes 1 | tf_op jit(solution)/shard_map/pallas_call | solution.py:48
  103.9 0.1 collective-permute-start.18
  103.9 0.5 collective-permute-start.19
  104.4 1.9 collective-permute-start.16
  106.4 6.5 %collective-permute-done.20.refs_9_ = bf16[4,32,2560]{2,1,0:T(8,128)(2,1)S(1)} collective-permute-done((bf16[4,32,2560]{2,1,0:T(8,128)(2,1)S(1)}, bf16[4,32,2560]{2,1,0:T(8,128)(2,1)S(1)}, u32[]{:S(2)}, u32[]{:S(2)}) %collective-permute-start.20) | collective-permute-done | bytes 655392 | tf_op jit(solution)/shard_map/ppermute | solution.py:233
  112.9 4.0 %collective-permute-start.17 = (bf16[4,32,2816]{2,1,0:T(8,128)(2,1)S(1)}, bf16[4,32,2816]{2,1,0:T(8,128)(2,1)S(1)}, u32[]{:S(2)}, u32[]{:S(2)}) collective-permute-start(bf16[4,32,2816]{2,1,0:T(8,128)(2,1)S(1)} %get-tuple-element.78.refs_11_), channel_id=1, source_target_pairs={{4,0},{8,4},{12,8},{16,12},{20,16},{24,20},{28,24},{5,1},{9,5},{13... | collective-permute-start | bytes 2162696 | tf_op jit(solution)/shard_map/ppermute | solution.py:234
  116.8 15.3 %collective-permute-done.21.refs_10_ = bf16[4,32,2560]{2,1,0:T(8,128)(2,1)S(1)} collective-permute-done((bf16[4,32,2560]{2,1,0:T(8,128)(2,1)S(1)}, bf16[4,32,2560]{2,1,0:T(8,128)(2,1)S(1)}, u32[]{:S(2)}, u32[]{:S(2)}) %collective-permute-start.21) | collective-permute-done | bytes 655392 | tf_op jit(solution)/shard_map/ppermute | solution.py:234
  132.2 5.0 %shard_map.59.refs_4_.refs_5_.refs_1_ = bf16[4,128,2816]{2,1,0:T(8,128)(2,1)S(1)} custom-call(bf16[4,384,192]{2,1,0:T(8,128)(2,1)S(1)} %get-tuple-element.62.refs_5_.refs_0_, f32[128,1]{1,0:T(8,128)S(1)} %tile.13.refs_4_.refs_1_, bf16[4,128,1280]{2,1,0:T(8,128)(2,1)S(1)} %copy-done.4, bf16[4,32,1280]{2,1,0:T(8,128)(2,1)S(1)} %collective-permute-done.4.refs_2_.refs_3_, ...), custom_call_target="tpu_custom_call" | custom-call | flops 99999997952 | bytes 1 | tf_op jit(solution)/shard_map/pallas_call | solution.py:48
  137.2 2.9 %shard_map.60 = (bf16[4,128,2560]{2,1,0:T(8,128)(2,1)S(1)}, bf16[4,32,2560]{2,1,0:T(8,128)(2,1)S(1)}, bf16[4,32,2560]{2,1,0:T(8,128)(2,1)S(1)}, bf16[128,2816]{1,0:T(8,128)(2,1)S(1)}, bf16[128,2816]{1,0:T(8,128)(2,1)S(1)}) custom-call(bf16[128,384]{1,0:T(8,128)(2,1)S(1)} %get-tuple-element.51.refs_3_.refs_0_, ...), custom_call_target="tpu_custom_call" | custom-call | flops 1000000 | bytes 1 | tf_op jit(solution)/shard_map/pallas_call | solution.py:48
  140.2 1.2 collective-permute-start.24
  141.4 1.9 collective-permute-start.22
  143.3 0.4 collective-permute-done.16.refs_3_
  143.8 4.0 %collective-permute-start.23 = (bf16[4,32,2560]{2,1,0:T(8,128)(2,1)S(1)}, bf16[4,32,2560]{2,1,0:T(8,128)(2,1)S(1)}, u32[]{:S(2)}, u32[]{:S(2)}) collective-permute-start(bf16[4,32,2560]{2,1,0:T(8,128)(2,1)S(1)} %get-tuple-element.85.refs_5_), channel_id=1, source_target_pairs={{4,0},{8,4},{12,8},{16,12},{20,16},{24,20},{28,24},{5,1},{9,5},{13... | collective-permute-start | bytes 1966088 | tf_op jit(solution)/shard_map/ppermute | solution.py:234
  147.7 13.9 %collective-permute-done.17.refs_4_ = bf16[4,32,2816]{2,1,0:T(8,128)(2,1)S(1)} collective-permute-done((bf16[4,32,2816]{2,1,0:T(8,128)(2,1)S(1)}, bf16[4,32,2816]{2,1,0:T(8,128)(2,1)S(1)}, u32[]{:S(2)}, u32[]{:S(2)}) %collective-permute-start.17) | collective-permute-done | bytes 720928 | tf_op jit(solution)/shard_map/ppermute | solution.py:234
  161.7 6.0 %shard_map.62.refs_8_ = bf16[4,32,4,8192]{3,2,1,0:T(4,128)(2,1)} custom-call(bf16[4,384,192]{2,1,0:T(8,128)(2,1)S(1)} %get-tuple-element.61.refs_0_, f32[128,1]{1,0:T(8,128)S(1)} %copy-done.1, bf16[4,128,2816]{2,1,0:T(8,128)(2,1)S(1)} %get-tuple-element.76.refs_2_, bf16[4,32,2816]{2,1,0:T(8,128)(2,1)S(1)} %collective-permute-done.16.refs_3_, ...), custom_call_target="tpu_custom_call" | custom-call | flops 99999997952 | bytes 1 | tf_op jit(solution)/shard_map/pallas_call | solution.py:48
  167.6 2.8 %shard_map.61 = (bf16[4,128,2816]{2,1,0:T(8,128)(2,1)S(1)}, bf16[4,32,2816]{2,1,0:T(8,128)(2,1)S(1)}, bf16[4,32,2816]{2,1,0:T(8,128)(2,1)S(1)}) custom-call(bf16[128,384]{1,0:T(8,128)(2,1)S(1)} %get-tuple-element.51.refs_3_.refs_0_, bf16[4,128,2816]{2,1,0:T(8,128)(2,1)S(1)} %shard_map.59.refs_4_.refs_5_.refs_1_, ...), custom_call_target="tpu_custom_call" | custom-call | flops 1000000 | bytes 1 | tf_op jit(solution)/shard_map/pallas_call | solution.py:48
  170.5 1.9 collective-permute-start.26
  172.4 4.5 %collective-permute-start.27 = (bf16[4,32,2816]{2,1,0:T(8,128)(2,1)S(1)}, bf16[4,32,2816]{2,1,0:T(8,128)(2,1)S(1)}, u32[]{:S(2)}, u32[]{:S(2)}) collective-permute-start(bf16[4,32,2816]{2,1,0:T(8,128)(2,1)S(1)} %get-tuple-element.90.refs_9_), channel_id=1, source_target_pairs={{4,0},{8,4},{12,8},{16,12},{20,16},{24,20},{28,24},{5,1},{9,5},{13... | collective-permute-start | bytes 2162696 | tf_op jit(solution)/shard_map/ppermute | solution.py:234
  176.9 5.9 %shard_map.63.refs_11_ = bf16[4,32,4,8192]{3,2,1,0:T(4,128)(2,1)} custom-call(bf16[4,384,192]{2,1,0:T(8,128)(2,1)S(1)} %get-tuple-element.61.refs_0_, f32[128,1]{1,0:T(8,128)S(1)} %copy-done.1, bf16[4,128,2816]{2,1,0:T(8,128)(2,1)S(1)} %get-tuple-element.76.refs_2_, ...), custom_call_target="tpu_custom_call", output_to_operand_aliasing={{}: (8, {})} | custom-call | flops 99999997952 | bytes 1 | tf_op jit(solution)/shard_map/pallas_call | solution.py:48
  182.8 20.4 %collective-permute-done.26.refs_9_ = bf16[4,32,2816]{2,1,0:T(8,128)(2,1)S(1)} collective-permute-done((bf16[4,32,2816]{2,1,0:T(8,128)(2,1)S(1)}, bf16[4,32,2816]{2,1,0:T(8,128)(2,1)S(1)}, u32[]{:S(2)}, u32[]{:S(2)}) %collective-permute-start.26) | collective-permute-done | bytes 720928 | tf_op jit(solution)/shard_map/ppermute | solution.py:233
  203.2 3.6 %collective-permute-done.27.refs_10_ = bf16[4,32,2816]{2,1,0:T(8,128)(2,1)S(1)} collective-permute-done((bf16[4,32,2816]{2,1,0:T(8,128)(2,1)S(1)}, bf16[4,32,2816]{2,1,0:T(8,128)(2,1)S(1)}, u32[]{:S(2)}, u32[]{:S(2)}) %collective-permute-start.27) | collective-permute-done | bytes 720928 | tf_op jit(solution)/shard_map/ppermute | solution.py:234
  206.8 6.8 %shard_map.64 = bf16[4,32,4,8192]{3,2,1,0:T(4,128)(2,1)} custom-call(bf16[4,384,192]{2,1,0:T(8,128)(2,1)S(1)} %get-tuple-element.61.refs_0_, f32[128,1]{1,0:T(8,128)S(1)} %copy-done.1, bf16[4,128,2816]{2,1,0:T(8,128)(2,1)S(1)} %get-tuple-element.76.refs_2_, ...), custom_call_target="tpu_custom_call", output_to_operand_aliasing={{}: (11, {})} | custom-call | flops 99999997952 | bytes 1 | tf_op jit(solution)/shard_map/pallas_call | solution.py:48
  (30 shorter events, 0.1 us)
Async XLA Ops:
  0.0 2.0 copy-start.2
  0.0 2.2 %copy-start.6 = (f32[2,32]{1,0:T(2,128)S(1)}, f32[2,32]{1,0:T(2,128)}, u32[]{:S(2)}) copy-start(f32[2,32]{1,0:T(2,128)} %param.7) | copy-start | bytes 772
  1.2 6.5 %collective-permute-start = (bf16[32,4,1280]{2,1,0:T(4,128)(2,1)S(1)}, bf16[32,4,1280]{2,1,0:T(4,128)(2,1)S(1)}, u32[]{:S(2)}, u32[]{:S(2)}) collective-permute-start(bf16[32,4,1280]{2,1,0:T(4,128)(2,1)S(1)} %get-tuple-element.49.refs_0_), channel_id=1, source_target_pairs={{0,1},{1,2},{2,3},{3,0},{4,5},{5,6},{6,7},{7,4},{8,9},{9,10},{10,1... | collective-permute-start | bytes 983048 | tf_op jit(solution)/shard_map/ppermute | solution.py:233
  2.0 9.2 %collective-permute-start.1 = (bf16[32,4,1280]{2,1,0:T(4,128)(2,1)S(1)}, bf16[32,4,1280]{2,1,0:T(4,128)(2,1)S(1)}, u32[]{:S(2)}, u32[]{:S(2)}) collective-permute-start(bf16[32,4,1280]{2,1,0:T(4,128)(2,1)S(1)} %get-tuple-element.50.refs_1_), channel_id=1, source_target_pairs={{1,0},{2,1},{3,2},{0,3},{5,4},{6,5},{7,6},{4,7},{9,8},{10,9},{11,1... | collective-permute-start | bytes 983048 | tf_op jit(solution)/shard_map/ppermute | solution.py:234
  2.4 1.3 copy-start
  11.2 9.1 %collective-permute-start.2 = (bf16[32,4,1792]{2,1,0:T(4,128)(2,1)S(1)}, bf16[32,4,1792]{2,1,0:T(4,128)(2,1)S(1)}, u32[]{:S(2)}, u32[]{:S(2)}) collective-permute-start(bf16[32,4,1792]{2,1,0:T(4,128)(2,1)S(1)} %get-tuple-element.54), channel_id=1, source_target_pairs={{0,1},{1,2},{2,3},{3,0},{4,5},{5,6},{6,7},{7,4},{8,9},{9,10},{10,1... | collective-permute-start | bytes 1376264 | tf_op jit(solution)/shard_map/ppermute | solution.py:233
  11.2 12.3 %collective-permute-start.3 = (bf16[32,4,1792]{2,1,0:T(4,128)(2,1)S(1)}, bf16[32,4,1792]{2,1,0:T(4,128)(2,1)S(1)}, u32[]{:S(2)}, u32[]{:S(2)}) collective-permute-start(bf16[32,4,1792]{2,1,0:T(4,128)(2,1)S(1)} %get-tuple-element.55), channel_id=1, source_target_pairs={{1,0},{2,1},{3,2},{0,3},{5,4},{6,5},{7,6},{4,7},{9,8},{10,9},{11,1... | collective-permute-start | bytes 1376264 | tf_op jit(solution)/shard_map/ppermute | solution.py:234
  14.0 1.1 copy-start.3
  15.1 17.0 %collective-permute-start.5 = (bf16[4,32,1280]{2,1,0:T(8,128)(2,1)S(1)}, bf16[4,32,1280]{2,1,0:T(8,128)(2,1)S(1)}, u32[]{:S(2)}, u32[]{:S(2)}) collective-permute-start(bf16[4,32,1280]{2,1,0:T(8,128)(2,1)S(1)} %get-tuple-element.56.refs_5_), channel_id=1, source_target_pairs={{4,0},{8,4},{12,8},{16,12},{20,16},{24,20},{28,24},{5,1},{9,5},{13... | collective-permute-start | bytes 983048 | tf_op jit(solution)/shard_map/ppermute | solution.py:234
  18.1 15.4 %collective-permute-start.4 = (bf16[4,32,1280]{2,1,0:T(8,128)(2,1)S(1)}, bf16[4,32,1280]{2,1,0:T(8,128)(2,1)S(1)}, u32[]{:S(2)}, u32[]{:S(2)}) collective-permute-start(bf16[4,32,1280]{2,1,0:T(8,128)(2,1)S(1)} %get-tuple-element.59), channel_id=1, source_target_pairs={{0,4},{4,8},{8,12},{12,16},{16,20},{20,24},{24,28},{1,5},{5,9},{9,... | collective-permute-start | bytes 983048 | tf_op jit(solution)/shard_map/ppermute | solution.py:233
  20.3 19.4 %copy-start.5 = (bf16[2,9,32,32]{3,2,1,0:T(8,128)(2,1)S(1)}, bf16[2,9,32,32]{3,2,1,0:T(8,128)(2,1)}, u32[]{:S(2)}) copy-start(bf16[2,9,32,32]{3,2,1,0:T(8,128)(2,1)} %kernel_ref.1) | copy-start | bytes 110596
  27.1 14.8 %collective-permute-start.8 = (bf16[32,4,2560]{2,1,0:T(4,128)(2,1)S(1)}, bf16[32,4,2560]{2,1,0:T(4,128)(2,1)S(1)}, u32[]{:S(2)}, u32[]{:S(2)}) collective-permute-start(bf16[32,4,2560]{2,1,0:T(4,128)(2,1)S(1)} %get-tuple-element.66), channel_id=1, source_target_pairs={{0,1},{1,2},{2,3},{3,0},{4,5},{5,6},{6,7},{7,4},{8,9},{9,10},{10,1... | collective-permute-start | bytes 1966088 | tf_op jit(solution)/shard_map/ppermute | solution.py:233
  27.2 16.2 %collective-permute-start.9 = (bf16[32,4,2560]{2,1,0:T(4,128)(2,1)S(1)}, bf16[32,4,2560]{2,1,0:T(4,128)(2,1)S(1)}, u32[]{:S(2)}, u32[]{:S(2)}) collective-permute-start(bf16[32,4,2560]{2,1,0:T(4,128)(2,1)S(1)} %get-tuple-element.67), channel_id=1, source_target_pairs={{1,0},{2,1},{3,2},{0,3},{5,4},{6,5},{7,6},{4,7},{9,8},{10,9},{11,1... | collective-permute-start | bytes 1966088 | tf_op jit(solution)/shard_map/ppermute | solution.py:234
  33.5 23.3 %collective-permute-start.6 = (bf16[4,32,1792]{2,1,0:T(8,128)(2,1)S(1)}, bf16[4,32,1792]{2,1,0:T(8,128)(2,1)S(1)}, u32[]{:S(2)}, u32[]{:S(2)}) collective-permute-start(bf16[4,32,1792]{2,1,0:T(8,128)(2,1)S(1)} %get-tuple-element.65), channel_id=1, source_target_pairs={{0,4},{4,8},{8,12},{12,16},{16,20},{20,24},{24,28},{1,5},{5,9},{9,... | collective-permute-start | bytes 1376264 | tf_op jit(solution)/shard_map/ppermute | solution.py:233
  37.6 35.0 %collective-permute-start.7 = (bf16[4,32,1792]{2,1,0:T(8,128)(2,1)S(1)}, bf16[4,32,1792]{2,1,0:T(8,128)(2,1)S(1)}, u32[]{:S(2)}, u32[]{:S(2)}) collective-permute-start(bf16[4,32,1792]{2,1,0:T(8,128)(2,1)S(1)} %get-tuple-element.60.refs_0_), channel_id=1, source_target_pairs={{4,0},{8,4},{12,8},{16,12},{20,16},{24,20},{28,24},{5,1},{9,5},{13... | collective-permute-start | bytes 1376264 | tf_op jit(solution)/shard_map/ppermute | solution.py:234
  43.4 29.2 %copy-start.4 = (bf16[4,128,1280]{2,1,0:T(8,128)(2,1)S(1)}, bf16[4,128,1280]{2,1,0:T(8,128)(2,1)}, u32[]{:S(2)}) copy-start(bf16[4,128,1280]{2,1,0:T(8,128)(2,1)} %copy-done.3) | copy-start | bytes 3932164
  47.7 30.0 %collective-permute-start.10 = (bf16[32,4,2560]{2,1,0:T(4,128)(2,1)S(1)}, bf16[32,4,2560]{2,1,0:T(4,128)(2,1)S(1)}, u32[]{:S(2)}, u32[]{:S(2)}) collective-permute-start(bf16[32,4,2560]{2,1,0:T(4,128)(2,1)S(1)} %get-tuple-element.69), channel_id=1, source_target_pairs={{0,1},{1,2},{2,3},{3,0},{4,5},{5,6},{6,7},{7,4},{8,9},{9,10},{10,1... | collective-permute-start | bytes 1966088 | tf_op jit(solution)/shard_map/ppermute | solution.py:233
  48.0 29.7 %collective-permute-start.11 = (bf16[32,4,2560]{2,1,0:T(4,128)(2,1)S(1)}, bf16[32,4,2560]{2,1,0:T(4,128)(2,1)S(1)}, u32[]{:S(2)}, u32[]{:S(2)}) collective-permute-start(bf16[32,4,2560]{2,1,0:T(4,128)(2,1)S(1)} %get-tuple-element.70), channel_id=1, source_target_pairs={{1,0},{2,1},{3,2},{0,3},{5,4},{6,5},{7,6},{4,7},{9,8},{10,9},{11,1... | collective-permute-start | bytes 1966088 | tf_op jit(solution)/shard_map/ppermute | solution.py:234
  48.2 36.9 %collective-permute-start.14 = (bf16[4,32,2560]{2,1,0:T(8,128)(2,1)S(1)}, bf16[4,32,2560]{2,1,0:T(8,128)(2,1)S(1)}, u32[]{:S(2)}, u32[]{:S(2)}) collective-permute-start(bf16[4,32,2560]{2,1,0:T(8,128)(2,1)S(1)} %get-tuple-element.74), channel_id=1, source_target_pairs={{0,4},{4,8},{8,12},{12,16},{16,20},{20,24},{24,28},{1,5},{5,9},{9,... | collective-permute-start | bytes 1966088 | tf_op jit(solution)/shard_map/ppermute | solution.py:233
  56.8 32.8 %collective-permute-start.15 = (bf16[4,32,2560]{2,1,0:T(8,128)(2,1)S(1)}, bf16[4,32,2560]{2,1,0:T(8,128)(2,1)S(1)}, u32[]{:S(2)}, u32[]{:S(2)}) collective-permute-start(bf16[4,32,2560]{2,1,0:T(8,128)(2,1)S(1)} %get-tuple-element.68.refs_8_), channel_id=1, source_target_pairs={{4,0},{8,4},{12,8},{16,12},{20,16},{24,20},{28,24},{5,1},{9,5},{13... | collective-permute-start | bytes 1966088 | tf_op jit(solution)/shard_map/ppermute | solution.py:234
  82.0 15.9 %collective-permute-start.12 = (bf16[128,2816]{1,0:T(8,128)(2,1)S(1)}, bf16[128,2816]{1,0:T(8,128)(2,1)S(1)}, u32[]{:S(2)}, u32[]{:S(2)}) collective-permute-start(bf16[128,2816]{1,0:T(8,128)(2,1)S(1)} %get-tuple-element.71), channel_id=1, source_target_pairs={{0,1},{1,2},{2,3},{3,0},{4,5},{5,6},{6,7},{7,4},{8,9},{9,10},{10,1... | collective-permute-start | bytes 2162696 | tf_op jit(solution)/shard_map/ppermute | solution.py:233
  83.2 17.4 %collective-permute-start.13 = (bf16[128,2816]{1,0:T(8,128)(2,1)S(1)}, bf16[128,2816]{1,0:T(8,128)(2,1)S(1)}, u32[]{:S(2)}, u32[]{:S(2)}) collective-permute-start(bf16[128,2816]{1,0:T(8,128)(2,1)S(1)} %get-tuple-element.72), channel_id=1, source_target_pairs={{1,0},{2,1},{3,2},{0,3},{5,4},{6,5},{7,6},{4,7},{9,8},{10,9},{11,1... | collective-permute-start | bytes 2162696 | tf_op jit(solution)/shard_map/ppermute | solution.py:234
  83.2 29.6 %collective-permute-start.20 = (bf16[4,32,2560]{2,1,0:T(8,128)(2,1)S(1)}, bf16[4,32,2560]{2,1,0:T(8,128)(2,1)S(1)}, u32[]{:S(2)}, u32[]{:S(2)}) collective-permute-start(bf16[4,32,2560]{2,1,0:T(8,128)(2,1)S(1)} %get-tuple-element.82), channel_id=1, source_target_pairs={{0,4},{4,8},{8,12},{12,16},{16,20},{20,24},{24,28},{1,5},{5,9},{9,... | collective-permute-start | bytes 1966088 | tf_op jit(solution)/shard_map/ppermute | solution.py:233
  85.2 47.0 %collective-permute-start.21 = (bf16[4,32,2560]{2,1,0:T(8,128)(2,1)S(1)}, bf16[4,32,2560]{2,1,0:T(8,128)(2,1)S(1)}, u32[]{:S(2)}, u32[]{:S(2)}) collective-permute-start(bf16[4,32,2560]{2,1,0:T(8,128)(2,1)S(1)} %get-tuple-element.75.refs_8_), channel_id=1, source_target_pairs={{4,0},{8,4},{12,8},{16,12},{20,16},{24,20},{28,24},{5,1},{9,5},{13... | collective-permute-start | bytes 1966088 | tf_op jit(solution)/shard_map/ppermute | solution.py:234
  103.9 33.3 %collective-permute-start.18 = (bf16[128,2560]{1,0:T(8,128)(2,1)S(1)}, bf16[128,2560]{1,0:T(8,128)(2,1)S(1)}, u32[]{:S(2)}, u32[]{:S(2)}) collective-permute-start(bf16[128,2560]{1,0:T(8,128)(2,1)S(1)} %get-tuple-element.79), channel_id=1, source_target_pairs={{0,1},{1,2},{2,3},{3,0},{4,5},{5,6},{6,7},{7,4},{8,9},{9,10},{10,1... | collective-permute-start | bytes 1966088 | tf_op jit(solution)/shard_map/ppermute | solution.py:233
  103.9 33.3 %collective-permute-start.19 = (bf16[128,2560]{1,0:T(8,128)(2,1)S(1)}, bf16[128,2560]{1,0:T(8,128)(2,1)S(1)}, u32[]{:S(2)}, u32[]{:S(2)}) collective-permute-start(bf16[128,2560]{1,0:T(8,128)(2,1)S(1)} %get-tuple-element.80), channel_id=1, source_target_pairs={{1,0},{2,1},{3,2},{0,3},{5,4},{6,5},{7,6},{4,7},{9,8},{10,9},{11,1... | collective-permute-start | bytes 1966088 | tf_op jit(solution)/shard_map/ppermute | solution.py:234
  104.4 39.3 %collective-permute-start.16 = (bf16[4,32,2816]{2,1,0:T(8,128)(2,1)S(1)}, bf16[4,32,2816]{2,1,0:T(8,128)(2,1)S(1)}, u32[]{:S(2)}, u32[]{:S(2)}) collective-permute-start(bf16[4,32,2816]{2,1,0:T(8,128)(2,1)S(1)} %get-tuple-element.77), channel_id=1, source_target_pairs={{0,4},{4,8},{8,12},{12,16},{16,20},{20,24},{24,28},{1,5},{5,9},{9,... | collective-permute-start | bytes 2162696 | tf_op jit(solution)/shard_map/ppermute | solution.py:233
  112.9 48.8 %collective-permute-start.17 = (bf16[4,32,2816]{2,1,0:T(8,128)(2,1)S(1)}, bf16[4,32,2816]{2,1,0:T(8,128)(2,1)S(1)}, u32[]{:S(2)}, u32[]{:S(2)}) collective-permute-start(bf16[4,32,2816]{2,1,0:T(8,128)(2,1)S(1)} %get-tuple-element.78.refs_11_), channel_id=1, source_target_pairs={{4,0},{8,4},{12,8},{16,12},{20,16},{24,20},{28,24},{5,1},{9,5},{13... | collective-permute-start | bytes 2162696 | tf_op jit(solution)/shard_map/ppermute | solution.py:234
  137.2 24.5 %copy-start.1 = (f32[128,1]{1,0:T(8,128)S(1)}, f32[128,1]{1,0:T(8,128)}, u32[]{:S(2)}) copy-start(f32[128,1]{1,0:T(8,128)} %copy-done) | copy-start | bytes 1540
  140.2 27.5 %collective-permute-start.24 = (bf16[128,2816]{1,0:T(8,128)(2,1)S(1)}, bf16[128,2816]{1,0:T(8,128)(2,1)S(1)}, u32[]{:S(2)}, u32[]{:S(2)}) collective-permute-start(bf16[128,2816]{1,0:T(8,128)(2,1)S(1)} %get-tuple-element.86), channel_id=1, source_target_pairs={{0,1},{1,2},{2,3},{3,0},{4,5},{5,6},{6,7},{7,4},{8,9},{9,10},{10,1... | collective-permute-start | bytes 2162696 | tf_op jit(solution)/shard_map/ppermute | solution.py:233
  141.4 26.2 %collective-permute-start.25 = (bf16[128,2816]{1,0:T(8,128)(2,1)S(1)}, bf16[128,2816]{1,0:T(8,128)(2,1)S(1)}, u32[]{:S(2)}, u32[]{:S(2)}) collective-permute-start(bf16[128,2816]{1,0:T(8,128)(2,1)S(1)} %get-tuple-element.87), channel_id=1, source_target_pairs={{1,0},{2,1},{3,2},{0,3},{5,4},{6,5},{7,6},{4,7},{9,8},{10,9},{11,1... | collective-permute-start | bytes 2162696 | tf_op jit(solution)/shard_map/ppermute | solution.py:234
  141.4 35.5 %collective-permute-start.22 = (bf16[4,32,2560]{2,1,0:T(8,128)(2,1)S(1)}, bf16[4,32,2560]{2,1,0:T(8,128)(2,1)S(1)}, u32[]{:S(2)}, u32[]{:S(2)}) collective-permute-start(bf16[4,32,2560]{2,1,0:T(8,128)(2,1)S(1)} %get-tuple-element.84), channel_id=1, source_target_pairs={{0,4},{4,8},{8,12},{12,16},{16,20},{20,24},{24,28},{1,5},{5,9},{9,... | collective-permute-start | bytes 1966088 | tf_op jit(solution)/shard_map/ppermute | solution.py:233
  143.8 33.1 %collective-permute-start.23 = (bf16[4,32,2560]{2,1,0:T(8,128)(2,1)S(1)}, bf16[4,32,2560]{2,1,0:T(8,128)(2,1)S(1)}, u32[]{:S(2)}, u32[]{:S(2)}) collective-permute-start(bf16[4,32,2560]{2,1,0:T(8,128)(2,1)S(1)} %get-tuple-element.85.refs_5_), channel_id=1, source_target_pairs={{4,0},{8,4},{12,8},{16,12},{20,16},{24,20},{28,24},{5,1},{9,5},{13... | collective-permute-start | bytes 1966088 | tf_op jit(solution)/shard_map/ppermute | solution.py:234
  170.5 32.7 %collective-permute-start.26 = (bf16[4,32,2816]{2,1,0:T(8,128)(2,1)S(1)}, bf16[4,32,2816]{2,1,0:T(8,128)(2,1)S(1)}, u32[]{:S(2)}, u32[]{:S(2)}) collective-permute-start(bf16[4,32,2816]{2,1,0:T(8,128)(2,1)S(1)} %get-tuple-element.89), channel_id=1, source_target_pairs={{0,4},{4,8},{8,12},{12,16},{16,20},{20,24},{24,28},{1,5},{5,9},{9,... | collective-permute-start | bytes 2162696 | tf_op jit(solution)/shard_map/ppermute | solution.py:233
  172.4 34.4 %collective-permute-start.27 = (bf16[4,32,2816]{2,1,0:T(8,128)(2,1)S(1)}, bf16[4,32,2816]{2,1,0:T(8,128)(2,1)S(1)}, u32[]{:S(2)}, u32[]{:S(2)}) collective-permute-start(bf16[4,32,2816]{2,1,0:T(8,128)(2,1)S(1)} %get-tuple-element.90.refs_9_), channel_id=1, source_target_pairs={{4,0},{8,4},{12,8},{16,12},{20,16},{24,20},{28,24},{5,1},{9,5},{13... | collective-permute-start | bytes 2162696 | tf_op jit(solution)/shard_map/ppermute | solution.py:234
